TPU v7x, 128 devices: a whole 4x4x4 slice. The times are simulated.
128 devices in a mesh: lon: 16 (over z_lo, x, core), lat: 8 (over y, z_hi).
Axes of the slice: x: 4, y: 4, z: 4 (z_hi: 2, z_lo: 2; z = z_hi * 2 + z_lo), core: 2. Of those that a mesh axis runs over, the one named last changes fastest.
Arguments:
- trajectory: float32 [3, 32, 512, 2048], P(None, None, 'lat', 'lon'), may hold values from -6 to 6
- adjoint_in: float32 [3, 32, 512, 2048], P(None, None, 'lat', 'lon'), may hold values from -6 to 6
- cutoffs: int32 [2, 64], replicated, may hold values from 2 to 511
Outputs:
- adjoint_out: float32 [3, 32, 512, 2048], P(None, None, 'lat', 'lon')
All inputs are finite; a program needn't handle non-finite values.
Results may differ from a plain program's by a relative error of at most 0.0003.
Values sent between devices are 32-bit elements; how exact they have to be, the bound alone decides.
A program may use at most 128 MiB of HBM per device.

v0:
```python
import jax
import jax.numpy as jnp
from jax import lax
from jax.sharding import PartitionSpec as P

cx = 0.25
cy = 0.25
cg = 0.3
ca = 0.25


def padded(array, sides, width):
    for axis, dim in sides:
        devices, length = (lax.axis_size(axis), array.shape[dim])
        up = [(i, (i + 1) % devices) for i in range(devices)]
        down = [(j, i) for i, j in up]
        last = lax.slice_in_dim(array, length - width, length, axis=dim)
        initial = lax.slice_in_dim(array, 0, width, axis=dim)
        before = lax.ppermute(last, axis, up)
        after = lax.ppermute(initial, axis, down)
        array = jnp.concatenate([before, array, after], axis=dim)
    return array


def out_region(delta, state, rows, nlat):
    h_in, u_in, v_in = (delta[0], delta[1], delta[2])
    h_st, u_st, v_st = (state[0], state[1], state[2])
    east_u = 0.5 * (u_st[:, :, :-1] + u_st[:, :, 1:])
    east_h = 0.5 * (h_st[:, :, :-1] + h_st[:, :, 1:])
    flux_x = east_u * 0.5 * (h_in[:, :, :-1] + h_in[:, :, 1:]) + east_h * 0.5 * (
        u_in[:, :, :-1] + u_in[:, :, 1:]
    )
    valid = ((rows[:-1] >= 0) & (rows[1:] <= nlat - 1)).astype(jnp.float32)[None, :, None]
    north_v = 0.5 * (v_st[:, :-1, :] + v_st[:, 1:, :])
    north_h = 0.5 * (h_st[:, :-1, :] + h_st[:, 1:, :])
    flux_y = valid * (
        north_v * 0.5 * (h_in[:, :-1, :] + h_in[:, 1:, :])
        + north_h * 0.5 * (v_in[:, :-1, :] + v_in[:, 1:, :])
    )
    div_x = flux_x[:, 1:-1, 1:] - flux_x[:, 1:-1, :-1]
    div_y = flux_y[:, 1:, 1:-1] - flux_y[:, :-1, 1:-1]
    h_out = h_in[:, 1:-1, 1:-1] - cx * div_x - cy * div_y
    u_out = (
        u_in[:, 1:-1, 1:-1]
        - cg * (h_in[:, 1:-1, 2:] - h_in[:, 1:-1, :-2])
        - ca * u_st[:, 1:-1, 1:-1] * (u_in[:, 1:-1, 2:] - u_in[:, 1:-1, :-2])
    )
    v_out = (
        v_in[:, 1:-1, 1:-1]
        - cg * (h_in[:, 2:, 1:-1] - h_in[:, :-2, 1:-1])
        - ca * v_st[:, 1:-1, 1:-1] * (v_in[:, 2:, 1:-1] - v_in[:, :-2, 1:-1])
    )
    return jnp.stack([h_out, u_out, v_out], 0)


def fourier_columns(nlon, start, width):
    index = jnp.arange(nlon, dtype=jnp.int32)[:, None]
    column = start + jnp.arange(width, dtype=jnp.int32)[None, :]
    half = nlon // 2
    wave = jnp.where(column <= half, column, column - half)
    phase = index * wave % nlon
    angle = 2.0 * jnp.pi / nlon * phase.astype(jnp.float32)
    scale = jnp.sqrt(2.0 / nlon)
    table = jnp.where(
        column == 0,
        1.0 / jnp.sqrt(1.0 * nlon),
        jnp.where(
            column == half,
            jnp.cos(angle) / jnp.sqrt(1.0 * nlon),
            jnp.where(column < half, scale * jnp.cos(angle), scale * jnp.sin(angle)),
        ),
    )
    return (table, wave[0].astype(jnp.float32))


def filter_rows(rows, cut):
    nlon = rows.shape[1]
    blocks = 4
    width = nlon // blocks

    def add_block(total, block):
        table, wave = fourier_columns(nlon, block * width, width)
        spectrum = jnp.dot(rows, table, precision=lax.Precision.HIGHEST)
        damp = jnp.minimum(1.0, (cut[:, None] / jnp.maximum(wave, 1.0)[None, :]) ** 2)
        part_sum = lax.dot_general(
            spectrum * damp, table, (((1,), (1,)), ((), ())), precision=lax.Precision.HIGHEST
        )
        return (total + part_sum, None)

    result, unused = lax.scan(
        add_block, jnp.zeros(rows.shape, jnp.float32), jnp.arange(blocks, dtype=jnp.int32)
    )
    return result


def row_cutoffs(cut_table, side, row_index, rows_dev):
    chosen = jnp.where(side == 0, cut_table[0], cut_table[1]).astype(jnp.float32)
    within = row_index % rows_dev
    match = within[:, None] == jnp.arange(rows_dev, dtype=jnp.int32)[None, :]
    return jnp.sum(jnp.where(match, chosen[None, :], 0.0), axis=1)


def lat_mask(extended, lat_at, rows_dev, nlat, width):
    global_row = lat_at * rows_dev - width + jnp.arange(rows_dev + 2 * width, dtype=jnp.int32)
    keep = ((global_row >= 0) & (global_row < nlat)).astype(jnp.float32)
    return extended * keep[None, None, :, None]


def per_device(trajectory, adjoint_in, cutoffs):
    lat_count = lax.axis_size("lat")
    lat_at = lax.axis_index("lat")
    lon_at = lax.axis_index("lon")
    fields, levels, rows_dev, lon_dev = adjoint_in.shape
    nlat = rows_dev * lat_count
    total = fields * levels * rows_dev
    flat = adjoint_in.reshape(total, lon_dev)
    is_cap = (lat_at == 0) | (lat_at == lat_count - 1)
    state_ext = padded(trajectory, (("lon", 3), ("lat", 2)), 2)
    circles = lax.all_to_all(flat, "lon", split_axis=0, concat_axis=1, tiled=True)
    count = circles.shape[0]
    row_index = lon_at * count + jnp.arange(count, dtype=jnp.int32)
    side = jnp.where(lat_at == 0, 0, 1)
    cut = row_cutoffs(cutoffs, side, row_index, rows_dev)
    back = lax.all_to_all(filter_rows(circles, cut), "lon", split_axis=1, concat_axis=0, tiled=True)
    mu_flat = jnp.where(is_cap, back, flat)
    filtered = mu_flat.reshape(adjoint_in.shape)
    mu_ext = padded(filtered, (("lon", 3), ("lat", 2)), 1)
    mu_ext = lat_mask(mu_ext, lat_at, rows_dev, nlat, 1)
    rows_in = lat_at * rows_dev - 2 + jnp.arange(rows_dev + 4, dtype=jnp.int32)

    def forward(delta):
        return out_region(delta, state_ext, rows_in, nlat)

    unused, pull = jax.vjp(forward, jnp.zeros(state_ext.shape, jnp.float32))
    return pull(mu_ext)[0][:, :, 2:-2, 2:-2]


def solution(mesh):
    in_specs = (P(None, None, "lat", "lon"), P(None, None, "lat", "lon"), P())
    out_specs = P(None, None, "lat", "lon")
    return jax.shard_map(
        per_device, mesh=mesh, in_specs=in_specs, out_specs=out_specs, check_vma=False
    )
```

profile of v0, /device:TPU:1, one launch (start us, length us, event | category | flops | bytes accessed | tf_op | source)
XLA Modules:
  0.0 466.9 jit_solution(8380511558618677451)
XLA Ops:
  0.0 7.3 %all-to-all-start = ((f32[16,384,128]{2,1,0:T(8,128)}), f32[16,384,128]{2,1,0:T(8,128)S(1)}, u32[]{:S(2)}, u32[]{:S(2)}) async-start(f32[16,384,128]{2,1,0:T(8,128)} %bitcast.62), calls=%async_computation | async-start | bytes 6291456 | tf_op jit(solution)/shard_map/all_to_all | solution.py:119
  7.4 0.1 select_reduce_fusion
  7.5 41.8 %all-to-all-done = f32[16,384,128]{2,1,0:T(8,128)S(1)} async-done(((f32[16,384,128]{2,1,0:T(8,128)}), f32[16,384,128]{2,1,0:T(8,128)S(1)}, u32[]{:S(2)}, u32[]{:S(2)}) %all-to-all-start) | async-done | bytes 3145760 | tf_op jit(solution)/shard_map/all_to_all | solution.py:119
  49.3 2.3 copy.37
  51.6 2.4 copy.38
  54.0 254.7 %while.13 = (s32[]{:T(128)}, f32[384,2048]{1,0:T(8,128)}, s32[4]{0:T(128)S(1)}, f32[384,2048]{1,0:T(8,128)S(1)}, f32[384]{0:T(512)S(1)}, /*index=5*/s32[]{:T(128)}, s32[1]{0:T(128)}, s32[]{:T(128)}) while((s32[]{:T(128)}, f32[384,2048]{1,0:T(8,128)}, s32[4]{0:T(128)S(1)}, f32[384,2048]{1,0:T(8,128)S(1)}, f32[384]{0:T(512)S(1)}, ...), condition=%wide.region_2.3_spmd.clone, body=%wide.region_1.2_spmd.clone.sunk | while | flops 9707986944 | bytes 36192456 | solution.py:90
  54.0 0.7 dynamic_slice.9
  55.4 0.0 copy-start.7
  55.5 30.9 %fusion.58 = f32[384,512]{0,1:T(8,128)S(1)} fusion(f32[384,2048]{1,0:T(8,128)S(1)} %get-tuple-element.204, s32[512]{0:T(512)S(1)} %compare_select_fusion.2, pred[512]{0:T(512)(128)(4,1)S(1)} %get-tuple-element.183, pred[512]{0:T(512)(128)(4,1)S(1)} %get-tuple-element.184, pred[512]{0:T(512)(128)(4,1)S(1)} %fusion.57, ...), kind=kOutput, calls=%fused_computation.13.clone.1 | convolution fusion | flops 4853596160 | bytes 3939328 | tf_op jit(solution)/shard_map/while/body/eval_jaxpr/dot_general | solution.py:83
  86.3 27.6 %select_add_fusion.2 = f32[384,2048]{1,0:T(8,128)S(1)} fusion(f32[384,2048]{1,0:T(8,128)S(1)} %copy-done.7, f32[384,512]{0,1:T(8,128)S(1)} %fusion.58, s32[512]{0:T(512)S(1)} %compare_select_fusion.2, pred[512]{0:T(512)(128)(4,1)S(1)} %get-tuple-element.183, pred[512]{0:T(512)(128)(4,1)S(1)} %get-tuple-element.184, pred[512]{0:T(512)(128)(4,1)S(1)} %fusion.57, ...), kind=kOutput, calls=%fused_computation.10.clone.1 | convolution fusion | flops 4854382592 | bytes 7081473 | tf_op jit(solution)/shard_map/while/body/eval_jaxpr/dot_general | solution.py:85
  113.9 0.0 copy-start.8
  113.9 1.7 copy-done.8
  115.6 0.7 dynamic_slice.9
  117.0 0.0 copy-start.7
  117.0 30.9 %fusion.58 = f32[384,512]{0,1:T(8,128)S(1)} fusion(f32[384,2048]{1,0:T(8,128)S(1)} %get-tuple-element.204, s32[512]{0:T(512)S(1)} %compare_select_fusion.2, pred[512]{0:T(512)(128)(4,1)S(1)} %get-tuple-element.183, pred[512]{0:T(512)(128)(4,1)S(1)} %get-tuple-element.184, pred[512]{0:T(512)(128)(4,1)S(1)} %fusion.57, ...), kind=kOutput, calls=%fused_computation.13.clone.1 | convolution fusion | flops 4853596160 | bytes 3939328 | tf_op jit(solution)/shard_map/while/body/eval_jaxpr/dot_general | solution.py:83
  147.9 27.6 %select_add_fusion.2 = f32[384,2048]{1,0:T(8,128)S(1)} fusion(f32[384,2048]{1,0:T(8,128)S(1)} %copy-done.7, f32[384,512]{0,1:T(8,128)S(1)} %fusion.58, s32[512]{0:T(512)S(1)} %compare_select_fusion.2, pred[512]{0:T(512)(128)(4,1)S(1)} %get-tuple-element.183, pred[512]{0:T(512)(128)(4,1)S(1)} %get-tuple-element.184, pred[512]{0:T(512)(128)(4,1)S(1)} %fusion.57, ...), kind=kOutput, calls=%fused_computation.10.clone.1 | convolution fusion | flops 4854382592 | bytes 7081473 | tf_op jit(solution)/shard_map/while/body/eval_jaxpr/dot_general | solution.py:85
  175.4 0.0 copy-start.8
  175.5 1.7 copy-done.8
  177.1 0.7 dynamic_slice.9
  178.5 0.0 copy-start.7
  178.5 30.9 %fusion.58 = f32[384,512]{0,1:T(8,128)S(1)} fusion(f32[384,2048]{1,0:T(8,128)S(1)} %get-tuple-element.204, s32[512]{0:T(512)S(1)} %compare_select_fusion.2, pred[512]{0:T(512)(128)(4,1)S(1)} %get-tuple-element.183, pred[512]{0:T(512)(128)(4,1)S(1)} %get-tuple-element.184, pred[512]{0:T(512)(128)(4,1)S(1)} %fusion.57, ...), kind=kOutput, calls=%fused_computation.13.clone.1 | convolution fusion | flops 4853596160 | bytes 3939328 | tf_op jit(solution)/shard_map/while/body/eval_jaxpr/dot_general | solution.py:83
  209.4 27.6 %select_add_fusion.2 = f32[384,2048]{1,0:T(8,128)S(1)} fusion(f32[384,2048]{1,0:T(8,128)S(1)} %copy-done.7, f32[384,512]{0,1:T(8,128)S(1)} %fusion.58, s32[512]{0:T(512)S(1)} %compare_select_fusion.2, pred[512]{0:T(512)(128)(4,1)S(1)} %get-tuple-element.183, pred[512]{0:T(512)(128)(4,1)S(1)} %get-tuple-element.184, pred[512]{0:T(512)(128)(4,1)S(1)} %fusion.57, ...), kind=kOutput, calls=%fused_computation.10.clone.1 | convolution fusion | flops 4854382592 | bytes 7081473 | tf_op jit(solution)/shard_map/while/body/eval_jaxpr/dot_general | solution.py:85
  237.0 0.0 copy-start.8
  237.0 1.7 copy-done.8
  238.7 0.7 dynamic_slice.9
  240.1 30.9 %fusion.58 = f32[384,512]{0,1:T(8,128)S(1)} fusion(f32[384,2048]{1,0:T(8,128)S(1)} %get-tuple-element.204, s32[512]{0:T(512)S(1)} %compare_select_fusion.2, pred[512]{0:T(512)(128)(4,1)S(1)} %get-tuple-element.183, pred[512]{0:T(512)(128)(4,1)S(1)} %get-tuple-element.184, pred[512]{0:T(512)(128)(4,1)S(1)} %fusion.57, ...), kind=kOutput, calls=%fused_computation.13.clone.1 | convolution fusion | flops 4853596160 | bytes 3939328 | tf_op jit(solution)/shard_map/while/body/eval_jaxpr/dot_general | solution.py:83
  271.0 27.6 %select_add_fusion.2 = f32[384,2048]{1,0:T(8,128)S(1)} fusion(f32[384,2048]{1,0:T(8,128)S(1)} %copy-done.7, f32[384,512]{0,1:T(8,128)S(1)} %fusion.58, s32[512]{0:T(512)S(1)} %compare_select_fusion.2, pred[512]{0:T(512)(128)(4,1)S(1)} %get-tuple-element.183, pred[512]{0:T(512)(128)(4,1)S(1)} %get-tuple-element.184, pred[512]{0:T(512)(128)(4,1)S(1)} %fusion.57, ...), kind=kOutput, calls=%fused_computation.10.clone.1 | convolution fusion | flops 4854382592 | bytes 7081473 | tf_op jit(solution)/shard_map/while/body/eval_jaxpr/dot_general | solution.py:85
  298.5 0.0 copy-start.8
  298.5 1.7 copy-done.8
  308.7 3.6 copy.39
  312.3 5.1 %all-to-all-start.1 = ((f32[384,16,128]{0,2,1:T(8,128)}), f32[384,16,128]{0,2,1:T(8,128)}, u32[]{:S(2)}, u32[]{:S(2)}) async-start(f32[384,16,128]{0,2,1:T(8,128)} %bitcast.60), calls=%async_computation.1 | async-start | bytes 6291456 | tf_op jit(solution)/shard_map/all_to_all | solution.py:124
  317.4 3.8 fusion.46
  321.2 2.5 copy.46
  323.7 0.3 collective-permute-start.1
  324.0 2.5 copy.45
  326.5 2.0 collective-permute-start
  328.5 0.1 and_convert_fusion
  328.6 31.9 %collective-permute-done = f32[3,32,64,2]{2,1,3,0:T(8,128)S(1)} collective-permute-done((f32[3,32,64,2]{2,1,3,0:T(8,128)S(1)}, f32[3,32,64,2]{2,1,3,0:T(8,128)S(1)}, u32[]{:S(2)}, u32[]{:S(2)}) %collective-permute-start) | collective-permute-done | bytes 49184 | tf_op jit(solution)/shard_map/ppermute | solution.py:19
  360.4 2.3 copy.35
  362.7 2.3 copy.36
  365.0 2.8 pad_maximum_fusion.3
  367.8 3.3 collective-permute-start.2
  371.1 2.5 collective-permute-start.3
  373.6 3.6 copy.40
  377.1 2.6 broadcast_select_fusion
  379.7 3.7 fusion.45
  383.4 3.1 copy.41
  386.4 3.1 copy.42
  389.5 2.8 collective-permute-start.4
  392.3 7.5 %pad_maximum_fusion = f32[3,32,68,132]{3,2,1,0:T(8,128)} fusion(f32[3,32,2,132]{3,2,1,0:T(2,128)S(1)} %collective-permute-done.3, f32[3,32,64,2]{3,2,1,0:T(8,128)} %copy.36, f32[3,32,64,128]{3,2,1,0:T(8,128)} %param.5, f32[3,32,64,2]{3,2,1,0:T(8,128)} %copy.35, f32[3,32,2,132]{3,2,1,0:T(2,128)S(1)} %collective-permute-done.2), kind=kLoop, calls=%fused_computation.34 | loop fusion | flops 3446784 | bytes 6893568 | tf_op jit(solution)/shard_map/concatenate | solution.py:21
  399.8 3.0 copy.43
  402.8 3.0 copy.44
  405.8 2.0 pad_maximum_fusion.6
  407.9 0.9 collective-permute-start.6
  408.7 4.5 collective-permute-start.7
  413.3 3.6 slice_bitcast_fusion.3
  416.9 3.5 maximum_multiply_fusion
  420.4 3.2 slice_bitcast_fusion.4
  423.6 7.6 %fusion.41 = (f32[32,66,130]{2,1,0:T(8,128)}, f32[32,66,130]{2,1,0:T(8,128)}, f32[32,66,130]{2,1,0:T(8,128)}, f32[32,66,130]{2,1,0:T(8,128)}, f32[32,66,130]{2,1...) fusion(f32[3,32,66,130]{3,2,1,0:T(8,128)S(1)} %maximum_multiply, ...), kind=kLoop, calls=%fused_computation.90 | loop fusion | flops 4118400 | bytes 16473600 | tf_op jit(solution)/shard_map/transpose(jvp())/neg | solution.py:51
  431.3 4.0 fusion.30
  435.3 3.9 fusion.33
  439.2 5.9 %add_bitcast_fusion.2 = f32[1,32,68,132]{3,2,1,0:T(8,128)S(1)} fusion(f32[32,67,132]{2,1,0:T(8,128)} %get-tuple-element.140, f32[32,66,130]{2,1,0:T(8,128)} %get-tuple-element.134, f32[32,66,130]{2,1,0:T(8,128)} %get-tuple-element.117, f32[32,66,130]{2,1,0:T(8,128)S(1)} %copy-done.5), kind=kLoop, calls=%fused_computation.63 | loop fusion | flops 1148928 | bytes 5575680 | tf_op jit(solution)/shard_map/transpose(jvp())/broadcast_in_dim | solution.py:26
  445.2 16.3 %add_bitcast_fusion = (f32[1,32,68,132]{3,2,1,0:T(8,128)}, f32[1,32,68,132]{3,2,1,0:T(8,128)}) fusion(f32[32,68,131]{2,1,0:T(8,128)} %get-tuple-element.143, f32[32,67,132]{2,1,0:T(8,128)} %get-tuple-element.141, f32[32,66,130]{2,1,0:T(8,128)} %get-tuple-element.136, f32[32,66,130]{2,1,0:T(8,128)} %get-tuple-element.128, ...), kind=kLoop, calls=%fused_computation.60 | loop fusion | flops 3446784 | bytes 14496256 | tf_op jit(solution)/shard_map/transpose(jvp())/broadcast_in_dim | solution.py:26
  461.4 5.1 %pad_add_fusion = f32[3,32,64,128]{3,2,1,0:T(8,128)} fusion(f32[1,32,68,132]{3,2,1,0:T(8,128)} %get-tuple-element.148, f32[1,32,68,132]{3,2,1,0:T(8,128)} %get-tuple-element.149, f32[1,32,68,132]{3,2,1,0:T(8,128)S(1)} %add_bitcast_fusion.2), kind=kLoop, calls=%fused_computation.36 | loop fusion | flops 1572864 | bytes 6592512 | tf_op jit(solution)/shard_map/transpose(jvp())/add_any | solution.py:26
  (52 shorter events, 0.2 us)
Async XLA Ops:
  0.0 7.3 %copy-start.9 = (s32[2,64]{1,0:T(2,128)S(1)}, s32[2,64]{1,0:T(2,128)}, u32[]{:S(2)}) copy-start(s32[2,64]{1,0:T(2,128)} %param.7) | copy-start | bytes 1540
  0.0 49.3 %all-to-all-start = ((f32[16,384,128]{2,1,0:T(8,128)}), f32[16,384,128]{2,1,0:T(8,128)S(1)}, u32[]{:S(2)}, u32[]{:S(2)}) async-start(f32[16,384,128]{2,1,0:T(8,128)} %bitcast.62), calls=%async_computation | async-start | bytes 6291456 | tf_op jit(solution)/shard_map/all_to_all | solution.py:119
  55.4 30.9 %copy-start.7 = (f32[384,2048]{1,0:T(8,128)S(1)}, f32[384,2048]{1,0:T(8,128)}, u32[]{:S(2)}) copy-start(f32[384,2048]{1,0:T(8,128)} %get-tuple-element.194) | copy-start | bytes 9437188 | tf_op jit(solution)/shard_map/while
  113.9 1.7 copy-start.8
  117.0 30.9 %copy-start.7 = (f32[384,2048]{1,0:T(8,128)S(1)}, f32[384,2048]{1,0:T(8,128)}, u32[]{:S(2)}) copy-start(f32[384,2048]{1,0:T(8,128)} %get-tuple-element.194) | copy-start | bytes 9437188 | tf_op jit(solution)/shard_map/while
  175.4 1.7 copy-start.8
  178.5 30.9 %copy-start.7 = (f32[384,2048]{1,0:T(8,128)S(1)}, f32[384,2048]{1,0:T(8,128)}, u32[]{:S(2)}) copy-start(f32[384,2048]{1,0:T(8,128)} %get-tuple-element.194) | copy-start | bytes 9437188 | tf_op jit(solution)/shard_map/while
  237.0 1.7 copy-start.8
  240.1 30.9 %copy-start.7 = (f32[384,2048]{1,0:T(8,128)S(1)}, f32[384,2048]{1,0:T(8,128)}, u32[]{:S(2)}) copy-start(f32[384,2048]{1,0:T(8,128)} %get-tuple-element.194) | copy-start | bytes 9437188 | tf_op jit(solution)/shard_map/while
  298.5 1.7 copy-start.8
  312.3 5.1 %copy-start = (f32[3,32,64,128]{3,2,1,0:T(8,128)S(1)}, f32[3,32,64,128]{3,2,1,0:T(8,128)}, u32[]{:S(2)}) copy-start(f32[3,32,64,128]{3,2,1,0:T(8,128)} %param.5) | copy-start | bytes 9437188
  312.3 61.2 %all-to-all-start.1 = ((f32[384,16,128]{0,2,1:T(8,128)}), f32[384,16,128]{0,2,1:T(8,128)}, u32[]{:S(2)}, u32[]{:S(2)}) async-start(f32[384,16,128]{0,2,1:T(8,128)} %bitcast.60), calls=%async_computation.1 | async-start | bytes 6291456 | tf_op jit(solution)/shard_map/all_to_all | solution.py:124
  323.7 39.0 %collective-permute-start.1 = (f32[3,32,64,2]{2,1,3,0:T(8,128)S(1)}, f32[3,32,64,2]{2,1,3,0:T(8,128)S(1)}, u32[]{:S(2)}, u32[]{:S(2)}) collective-permute-start(f32[3,32,64,2]{2,1,3,0:T(8,128)S(1)} %copy.46), channel_id=1, source_target_pairs={{8,0},{16,8},{24,16},{32,24},{40,32},{48,40},{56,48},{64,56},{72,6... | collective-permute-start | bytes 147464 | tf_op jit(solution)/shard_map/ppermute | solution.py:20
  326.5 33.9 %collective-permute-start = (f32[3,32,64,2]{2,1,3,0:T(8,128)S(1)}, f32[3,32,64,2]{2,1,3,0:T(8,128)S(1)}, u32[]{:S(2)}, u32[]{:S(2)}) collective-permute-start(f32[3,32,64,2]{2,1,3,0:T(8,128)S(1)} %copy.45), channel_id=1, source_target_pairs={{0,8},{8,16},{16,24},{24,32},{32,40},{40,48},{48,56},{56,64},{64,7... | collective-permute-start | bytes 147464 | tf_op jit(solution)/shard_map/ppermute | solution.py:19
  367.8 24.5 %collective-permute-start.2 = (f32[3,32,2,132]{3,2,1,0:T(2,128)}, f32[3,32,2,132]{3,2,1,0:T(2,128)S(1)}, u32[]{:S(2)}, u32[]{:S(2)}) collective-permute-start(f32[3,32,2,132]{3,2,1,0:T(2,128)} %get-tuple-element.124), channel_id=1, source_target_pairs={{0,1},{1,2},{2,3},{3,4},{4,5},{5,6},{6,7},{7,0},{8,9},{9,10},{10,1... | collective-permute-start | bytes 304136 | tf_op jit(solution)/shard_map/ppermute | solution.py:19
  371.1 21.2 %collective-permute-start.3 = (f32[3,32,2,132]{3,2,1,0:T(2,128)}, f32[3,32,2,132]{3,2,1,0:T(2,128)S(1)}, u32[]{:S(2)}, u32[]{:S(2)}) collective-permute-start(f32[3,32,2,132]{3,2,1,0:T(2,128)} %get-tuple-element.125), channel_id=1, source_target_pairs={{1,0},{2,1},{3,2},{4,3},{5,4},{6,5},{7,6},{0,7},{9,8},{10,9},{11,1... | collective-permute-start | bytes 304136 | tf_op jit(solution)/shard_map/ppermute | solution.py:20
  389.5 13.3 %collective-permute-start.5 = (f32[3,32,64,1]{2,1,3,0:T(8,128)}, f32[3,32,64,1]{2,1,3,0:T(8,128)}, u32[]{:S(2)}, u32[]{:S(2)}) collective-permute-start(f32[3,32,64,1]{2,1,3,0:T(8,128)} %copy.42), channel_id=1, source_target_pairs={{8,0},{16,8},{24,16},{32,24},{40,32},{48,40},{56,48},{64,56},{72,6... | collective-permute-start | bytes 73736 | tf_op jit(solution)/shard_map/ppermute | solution.py:20
  389.5 10.3 %collective-permute-start.4 = (f32[3,32,64,1]{2,1,3,0:T(8,128)}, f32[3,32,64,1]{2,1,3,0:T(8,128)}, u32[]{:S(2)}, u32[]{:S(2)}) collective-permute-start(f32[3,32,64,1]{2,1,3,0:T(8,128)} %copy.41), channel_id=1, source_target_pairs={{0,8},{8,16},{16,24},{24,32},{32,40},{40,48},{48,56},{56,64},{64,7... | collective-permute-start | bytes 73736 | tf_op jit(solution)/shard_map/ppermute | solution.py:19
  407.9 9.0 %collective-permute-start.6 = (f32[3,32,1,130]{3,2,1,0:T(1,128)S(1)}, f32[3,32,1,130]{3,2,1,0:T(1,128)S(1)}, u32[]{:S(2)}, u32[]{:S(2)}) collective-permute-start(f32[3,32,1,130]{3,2,1,0:T(1,128)S(1)} %get-tuple-element.122), channel_id=1, source_target_pairs={{0,1},{1,2},{2,3},{3,4},{4,5},{5,6},{6,7},{7,0},{8,9},{9,10},{10,1... | collective-permute-start | bytes 149768 | tf_op jit(solution)/shard_map/ppermute | solution.py:19
  408.7 8.2 %copy-start.3 = (f32[3,32,64,1]{3,2,1,0:T(8,128)S(1)}, f32[3,32,64,1]{3,2,1,0:T(8,128)}, u32[]{:S(2)}) copy-start(f32[3,32,64,1]{3,2,1,0:T(8,128)} %copy.43) | copy-start | bytes 73732
  408.7 8.2 %copy-start.4 = (f32[3,32,64,1]{3,2,1,0:T(8,128)S(1)}, f32[3,32,64,1]{3,2,1,0:T(8,128)}, u32[]{:S(2)}) copy-start(f32[3,32,64,1]{3,2,1,0:T(8,128)} %copy.44) | copy-start | bytes 73732
  408.7 8.2 %collective-permute-start.7 = (f32[3,32,1,130]{3,2,1,0:T(1,128)S(1)}, f32[3,32,1,130]{3,2,1,0:T(1,128)S(1)}, u32[]{:S(2)}, u32[]{:S(2)}) collective-permute-start(f32[3,32,1,130]{3,2,1,0:T(1,128)S(1)} %get-tuple-element.123), channel_id=1, source_target_pairs={{1,0},{2,1},{3,2},{4,3},{5,4},{6,5},{7,6},{0,7},{9,8},{10,9},{11,1... | collective-permute-start | bytes 149768 | tf_op jit(solution)/shard_map/ppermute | solution.py:20
  416.9 6.8 %copy-start.1 = (f32[32,68,132]{2,1,0:T(8,128)}, f32[32,68,132]{2,1,0:T(8,128)S(1)}, u32[]{:S(2)}) copy-start(f32[32,68,132]{2,1,0:T(8,128)S(1)} %get-tuple-element.139) | copy-start | bytes 3446788
  431.3 4.1 copy-start.2
  435.3 3.9 copy-start.5
  439.2 5.9 %copy-start.6 = (f32[32,66,130]{2,1,0:T(8,128)S(1)}, f32[32,66,130]{2,1,0:T(8,128)}, u32[]{:S(2)}) copy-start(f32[32,66,130]{2,1,0:T(8,128)} %get-tuple-element.126) | copy-start | bytes 3294724
where the time goes:
time: 467 us
  matrix products  234 us (50%)
  waiting for transfers between devices  73.7 us (16%)
  other arithmetic  61.6 us (13%)
  local copies, waits for them, and re-layouts  57.1 us (12%)
  starting transfers between devices  28.6 us (6%)
  loops' own time  11.6 us (2%)
    dot_general x4, matrix products, add_block(): spectrum = jnp.dot(rows, table, precision=lax.Precision.HIGHEST)  123 us
    dot_general x4, matrix products, add_block(): lax.dot_general(spectrum * damp, table, (((1,), (1,)), ((), ())), precisi...  110 us
    all_to_all x1, waiting for transfers between devices, per_device(): lax.all_to_all(flat, 'lon', split_axis=0, concat_axis=1, tiled=True)  41.8 us
    ppermute x4, waiting for transfers between devices, padded(): before = lax.ppermute(last, axis, up)  31.9 us
    broadcast_in_dim x2, other arithmetic, out_region(): h_in, u_in, v_in = (delta[0], delta[1], delta[2])  22.2 us
    another operation x1, loops' own time, filter_rows(): lax.scan(add_block, jnp.zeros(rows.shape, jnp.float32), jnp.arange(blocks...  11.6 us
    slice x3, local copies, waits for them, and re-layouts, padded(): last = lax.slice_in_dim(array, length - width, length, axis=dim)  10.6 us
  transfers between devices with their start and end apart: 10, of which 2 were waited for; matrix products, arithmetic and copies ran while one was open for 10% of the time, Pallas kernels for 0%

commit v1 on v0

v1 whole, which is shorter than its diff:
```python
import functools

import jax
import jax.numpy as jnp
import ml_dtypes
import numpy as np
from jax import lax
from jax.experimental import pallas as pl
from jax.experimental.pallas import tpu as pltpu
from jax.sharding import PartitionSpec as P

MESH = pl.DeviceIdType.MESH
NLON, LEV, ROWS, LANES, LON, LAT = 2048, 32, 64, 128, 16, 8
PAIRS = 3 * LEV
HALF, CHUNKS = 32, 12
HOME, SINGLE, EACH = 5, 3, 2
SLOTS = 5
cx, cy, cg, ca = 0.25, 0.25, 0.3, 0.25


def tables():
    m = np.arange(LANES)[:, None]
    k = np.arange(LANES)[None, :]
    forward = np.zeros((8, 256, 256))
    inverse = np.zeros((8, 256, 256))
    wave = np.zeros((8, 256))

    def angle(freq):
        return 2.0 * np.pi / NLON * ((freq * m) % NLON)

    for q in range(1, 8):
        freq = 16 * k + q
        cos, sin = np.cos(angle(freq)), np.sin(angle(freq))
        forward[q] = np.block([[cos, -sin], [sin, cos]])
        inverse[q] = forward[q].T / NLON
        wave[q] = np.tile(np.minimum(freq, NLON - freq)[0], 2)
    index = np.arange(LANES)
    for at, q, is_cos, order in (
        (0, 0, index <= 64, np.where(index <= 64, index, index - 64)),
        (128, 8, index < 64, index % 64),
    ):
        freq = (16 * order + q)[None, :]
        block = np.where(is_cos[None, :], np.cos(angle(freq)), -np.sin(angle(freq)))
        weight = np.where((freq == 0) | (freq == NLON // 2), 1.0, 2.0)
        forward[0, at : at + 128, at : at + 128] = block
        inverse[0, at : at + 128, at : at + 128] = (block * weight).T / NLON
        wave[0, at : at + 128] = freq[0]
    both = np.stack([forward, inverse])
    high = both.astype(np.float32).astype(ml_dtypes.bfloat16)
    low = (both - high.astype(np.float64)).astype(np.float32).astype(ml_dtypes.bfloat16)
    damp = (1.0 / np.maximum(wave, 1.0) ** 2).astype(np.float32)
    return np.stack([high, low], 1), damp


def cadd(a, b, sign=1.0):
    re = a[0] + b[0] if sign > 0 else a[0] - b[0]
    if a[1] is None and b[1] is None:
        return (re, None)
    if a[1] is None:
        return (re, b[1] if sign > 0 else -b[1])
    if b[1] is None:
        return (re, a[1])
    return (re, a[1] + b[1] if sign > 0 else a[1] - b[1])


def conj(a):
    return a if a[1] is None else (a[0], -a[1])


def ctwist(a, k, n, sign):
    if k == 0:
        return a
    re, im = a
    if 4 * k == n:
        if im is None:
            return (jnp.zeros_like(re), re if sign > 0 else -re)
        return (-im, re) if sign > 0 else (im, -re)
    c, s = float(np.cos(2 * np.pi * k / n)), sign * float(np.sin(2 * np.pi * k / n))
    if im is None:
        return (re * c, re * s)
    if 8 * k == n:
        return ((re - im) * c, (re + im) * c) if sign > 0 else ((re + im) * c, (im - re) * c)
    return (re * c - im * s, re * s + im * c)


def real_dft(xs):
    n = len(xs)
    if n == 1:
        return [(xs[0], None)]
    if n == 2:
        return [(xs[0] + xs[1], None), (xs[0] - xs[1], None)]
    even, odd = real_dft(xs[0::2]), real_dft(xs[1::2])
    out = [None] * (n // 2 + 1)
    for k in range(n // 4 + 1):
        turned = ctwist(odd[k], k, n, -1)
        out[k] = cadd(even[k], turned)
        if k != n // 4:
            out[n // 2 - k] = conj(cadd(even[k], turned, -1.0))
    return out


def real_inverse(spec):
    n = 2 * (len(spec) - 1)
    if n == 2:
        return [spec[0][0] + spec[1][0], spec[0][0] - spec[1][0]]
    even, odd = [], []
    for k in range(n // 4 + 1):
        other = conj(spec[n // 2 - k])
        even.append(cadd(spec[k], other))
        odd.append(ctwist(cadd(spec[k], other, -1.0), k, n, 1))
    for part in (even, odd):
        part[0] = (part[0][0], None)
        part[-1] = (part[-1][0], None)
    a, b = real_inverse(even), real_inverse(odd)
    return [v for both in zip(a, b) for v in both]


def product(z, high, low):
    hi = z.astype(jnp.bfloat16)
    lo = (z - hi.astype(jnp.float32)).astype(jnp.bfloat16)
    rows = z.shape[0]
    main = jnp.dot(jnp.concatenate([hi, lo], 0), high, preferred_element_type=jnp.float32)
    rest = jnp.dot(hi, low, preferred_element_type=jnp.float32)
    return main[:rows] + main[rows:] + rest


def filter_chunk(blocks, table, damp_of):
    spec = real_dft(blocks)
    groups = [jnp.concatenate([spec[0][0], spec[8][0]], 1)]
    groups += [jnp.concatenate(spec[q], 1) for q in range(1, 8)]
    back = []
    for q in range(8):
        waves = product(groups[q], table[0, 0, q], table[0, 1, q]) * damp_of(q)
        back.append(product(waves, table[1, 0, q], table[1, 1, q]))
    spec = [(back[0][:, :LANES], None)]
    spec += [(back[q][:, :LANES], back[q][:, LANES:]) for q in range(1, 8)]
    spec += [(back[0][:, LANES:], None)]
    return real_inverse(spec)


def flip_bits(value, mask, width=4):
    out = 0
    for bit in range(width):
        own = (value // (1 << bit)) % 2
        out = out + (1 << bit) * ((1 - own) if (mask >> bit) & 1 else own)
    return out


def exchange_kernel(
    adj, traj, cuts, inverse_k2, table_in,
    mu_out, ewt_out, ewm_out, ns_out,
    mu, trj, rin, rcv, yout, rout, table, damp, ew_send, ew_recv, ns_send, ns_recv,
    rin_sem, relay_sem, fs_sem, rcv_sem, bs_sem, rout_sem, ro_sem, mu_sem,
    ews_sem, ewr_sem, nss_sem, nsr_sem, local_sem,
):
    lon = lax.axis_index("lon")
    lat = lax.axis_index("lat")
    mirror = flip_bits(lon, 8)
    is_cap = (lat == 0) | (lat == LAT - 1)
    is_single = (lat == 2) | (lat == 5)
    is_double = (lat == 1) | (lat == 6)
    steps = jnp.where(is_cap, HOME, jnp.where(is_single, SINGLE, jnp.where(is_double, 2 * EACH, 0)))
    lower = lat < LAT // 2

    def to(lon_at, lat_at):
        return {"lon": lon_at, "lat": lat_at}

    peers = [to(flip_bits(lon, k), lat) for k in range(1, 16)]
    peers += [to(lon, (lat + k) % LAT) for k in (1, 2, 6, 7)]
    peers += [to(mirror, flip_bits(lat, 1, 3))]
    barrier = pltpu.get_barrier_semaphore()
    for peer in peers:
        pl.semaphore_signal(barrier, inc=1, device_id=peer, device_id_type=MESH)

    table_copy = pltpu.make_async_copy(table_in, table, local_sem.at[0])
    traj_copy = pltpu.make_async_copy(traj, trj, local_sem.at[1])
    mu_copy = pltpu.make_async_copy(adj, mu, local_sem.at[2])
    traj_copy.start()
    table_copy.start()

    @pl.when(jnp.logical_not(is_cap))
    def _():
        mu_copy.start()

    pl.semaphore_wait(barrier, len(peers))

    def chunk_of(ref, chunk):
        pair = pl.multiple_of(16 * (chunk // 2), 16)
        row = pl.multiple_of(HALF * (chunk % 2), HALF)
        return ref.at[pl.ds(pair, 16), pl.ds(row, HALF)]

    def relay(chunk, device, slot):
        pltpu.make_async_remote_copy(
            src_ref=chunk_of(adj, chunk), dst_ref=rin.at[slot],
            send_sem=relay_sem.at[chunk], recv_sem=rin_sem.at[slot],
            device_id=device, device_id_type=MESH,
        ).start()

    def step_of(s):
        odd = s % 2
        near, far = jnp.where(lower, 0, LAT - 1), jnp.where(lower, LAT - 1, 0)
        cap = jnp.where(is_double & (odd == 1), far, near)
        chunk = jnp.where(
            is_cap, s, jnp.where(is_single, HOME + s, HOME + SINGLE + EACH * odd + s // 2)
        )
        flip = jnp.where(is_double & (odd == 0), 1, 0)
        return cap, chunk, flip

    def all_to_all(src_at, dst_at, send_sem, recv_sem):
        for k in range(1, 16):
            member = flip_bits(lon, k)
            pltpu.make_async_remote_copy(
                src_ref=src_at(member), dst_ref=dst_at, send_sem=send_sem, recv_sem=recv_sem,
                device_id=to(member, lat), device_id_type=MESH,
            ).start()
        pltpu.make_async_copy(src_at(lon), dst_at, recv_sem).start()

    def home_lon(member, flip):
        return jnp.where(flip == 1, (member + 8) % 16, member)

    def forward(s):
        unused_cap, unused_chunk, flip = step_of(s)
        pltpu.make_async_copy(rin.at[s], rin.at[s], rin_sem.at[s]).wait()
        all_to_all(
            lambda member: rin.at[s, member], rcv.at[s, home_lon(lon, flip)], fs_sem.at[s], rcv_sem.at[s]
        )

    def backward(s):
        unused_cap, unused_chunk, flip = step_of(s)
        all_to_all(
            lambda member: yout.at[s, home_lon(member, flip)], rout.at[s, lon], bs_sem.at[s], rout_sem.at[s]
        )

    def work(s):
        cap, chunk, unused_flip = step_of(s)
        side = jnp.where(cap == 0, 0, 1)
        row = pl.multiple_of(HALF * (chunk % 2), HALF)
        pltpu.make_async_copy(rcv.at[s], rcv.at[s], rcv_sem.at[s]).wait()
        done = filter_chunk(
            [rcv[s, d] for d in range(16)], table, lambda q: damp[side, q, pl.ds(row, HALF), :]
        )
        for d in range(16):
            yout[s, d] = done[d]

    def deliver(s):
        cap, chunk, flip = step_of(s)
        pltpu.make_async_copy(rout.at[s], rout.at[s], rout_sem.at[s]).wait()

        @pl.when(is_cap)
        def _():
            pltpu.make_async_copy(rout.at[s], chunk_of(mu, chunk), mu_sem.at[chunk]).start()

        @pl.when(jnp.logical_not(is_cap))
        def _():
            pltpu.make_async_remote_copy(
                src_ref=rout.at[s], dst_ref=chunk_of(mu, chunk),
                send_sem=ro_sem.at[s], recv_sem=mu_sem.at[chunk],
                device_id=to(home_lon(lon, flip), cap), device_id_type=MESH,
            ).start()

    @pl.when(is_cap)
    def _():
        turn = jnp.where(lower, 2, LAT - 2)
        single, other = (lat + turn) % LAT, (lat + LAT - turn) % LAT
        for s in range(HOME):
            pltpu.make_async_copy(chunk_of(adj, s), rin.at[s], rin_sem.at[s]).start()
        for s in range(SINGLE):
            relay(HOME + s, to(lon, single), s)
            if s < EACH:
                relay(HOME + SINGLE + s, to(mirror, flip_bits(lat, 1, 3)), 2 * s)
                relay(HOME + SINGLE + EACH + s, to(lon, other), 2 * s + 1)

        @pl.loop(0, HOME)
        def _(s):
            forward(s)

    lane = lax.broadcasted_iota(jnp.int32, (ROWS, LANES), 1)

    def pack(ref, kind, other_field):
        def body(level, packed):
            west, east = packed
            for at, f in ((0, 0), (LEV, other_field)):
                target = at + level
                turned = pltpu.roll(ref[f * LEV + level], target, axis=1)
                west = jnp.where(lane == target, turned, west)
                east = jnp.where(lane == (target + LANES - 1) % LANES, turned, east)
            return west, east

        zero = jnp.zeros((ROWS, LANES), jnp.float32)
        west, east = lax.fori_loop(0, LEV, body, (zero, zero))
        ew_send[kind, 0] = west
        ew_send[kind, 1] = east

    def pack_rows(ref, kind):
        for at, f in ((0, 0), (LEV, 2)):
            @pl.loop(0, LEV)
            def _(level):
                ns_send[kind, 0, pl.ds(at + level, 1), :] = ref[f * LEV + level, 0:1, :]
                ns_send[kind, 1, pl.ds(at + level, 1), :] = ref[f * LEV + level, ROWS - 1 : ROWS, :]

    def halo_copies(kind):
        ew, ns = [], []
        for side, step in ((0, LON - 1), (1, 1)):
            ew.append(pltpu.make_async_remote_copy(
                src_ref=ew_send.at[kind, side], dst_ref=ew_recv.at[kind, 1 - side],
                send_sem=ews_sem.at[kind, side], recv_sem=ewr_sem.at[kind, 1 - side],
                device_id=to((lon + step) % LON, lat), device_id_type=MESH,
            ))
        for side, step in ((0, LAT - 1), (1, 1)):
            ns.append(pltpu.make_async_remote_copy(
                src_ref=ns_send.at[kind, side], dst_ref=ns_recv.at[kind, 1 - side],
                send_sem=nss_sem.at[kind, side], recv_sem=nsr_sem.at[kind, 1 - side],
                device_id=to(lon, (lat + step) % LAT), device_id_type=MESH,
            ))
        return ew, ns

    def send_halos(ref, kind, ew_field):
        pack(ref, kind, ew_field)
        pack_rows(ref, kind)
        ew, ns = halo_copies(kind)
        ew[0].start()
        ew[1].start()

        @pl.when(lat > 0)
        def _():
            ns[0].start()

        @pl.when(lat < LAT - 1)
        def _():
            ns[1].start()

    traj_copy.wait()
    send_halos(trj, 0, 1)

    @pl.when(jnp.logical_not(is_cap))
    def _():
        mu_copy.wait()
        send_halos(mu, 1, 1)

    row_at = lax.broadcasted_iota(jnp.int32, (ROWS, ROWS), 0)
    col_at = lax.broadcasted_iota(jnp.int32, (ROWS, ROWS), 1)
    for side in range(2):
        cut = cuts[side : side + 1, :].astype(jnp.float32)
        column = jnp.sum(jnp.where(row_at == col_at, cut, 0.0), axis=1, keepdims=True)
        for q in range(8):
            damp[side, q] = jnp.minimum(1.0, column * column * inverse_k2[q : q + 1, :])
    table_copy.wait()

    @pl.loop(0, steps + 2)
    def _(t):
        @pl.when(jnp.logical_not(is_cap) & (t < steps))
        def _():
            forward(t)

        @pl.when((t >= 1) & (t <= steps))
        def _():
            work(t - 1)
            backward(t - 1)

        @pl.when((t >= 2) & (steps > 0))
        def _():
            deliver(t - 2)

    @pl.when(is_cap)
    def _():
        for chunk in range(CHUNKS):
            part = chunk_of(mu, chunk)
            pltpu.make_async_copy(part, part, mu_sem.at[chunk]).wait()
        send_halos(mu, 1, 1)

    out_copy = pltpu.make_async_copy(mu, mu_out, local_sem.at[3])
    out_copy.start()

    @pl.when(is_cap)
    def _():
        for chunk in range(HOME, CHUNKS):
            part = chunk_of(mu, chunk)
            pltpu.make_async_copy(part, part, relay_sem.at[chunk]).wait()

    @pl.loop(0, steps)
    def _(s):
        most = rin.at[s, pl.ds(0, 15)]
        pltpu.make_async_copy(most, most, fs_sem.at[s]).wait()
        pltpu.make_async_copy(most, most, bs_sem.at[s]).wait()

        @pl.when(jnp.logical_not(is_cap))
        def _():
            pltpu.make_async_copy(rin.at[s], rin.at[s], ro_sem.at[s]).wait()

    for kind in range(2):
        ew, ns = halo_copies(kind)
        ew[0].wait()
        ew[1].wait()
        for side, here in ((0, lat > 0), (1, lat < LAT - 1)):
            @pl.when(here)
            def _():
                ns[side].wait_send()
                whole = ns_recv.at[kind, side]
                pltpu.make_async_copy(whole, whole, nsr_sem.at[kind, side]).wait()
                ns_out[kind, side] = ns_recv[kind, side]

            @pl.when(jnp.logical_not(here))
            def _():
                ns_out[kind, side] = jnp.zeros((2 * LEV, LANES), jnp.float32)

    ewt_out[...] = ew_recv[0]
    ewm_out[...] = ew_recv[1]
    out_copy.wait()


LEVELS_STEP = 4


def stencil_kernel(traj, mu, ewt, ewm, ns, out):
    lat = lax.axis_index("lat")
    first = pl.program_id(0) * LEVELS_STEP
    row = lax.broadcasted_iota(jnp.int32, (ROWS, LANES), 0)
    lane = lax.broadcasted_iota(jnp.int32, (ROWS, LANES), 1)
    no_south = (row == 0) & (lat == 0)
    no_north = (row == ROWS - 1) & (lat == LAT - 1)

    def level_step(j, unused):
        level = first + j

        def east_west(x, halo, at):
            from_west = jnp.where(lane == LANES - 1, pltpu.roll(halo[0], (2 * LANES - at) % LANES, axis=1), x)
            from_east = jnp.where(lane == 0, pltpu.roll(halo[1], (2 * LANES - at) % LANES, axis=1), x)
            return pltpu.roll(from_west, 1, axis=1), pltpu.roll(from_east, LANES - 1, axis=1)

        def south_north(x, kind, at):
            south = jnp.broadcast_to(ns[kind, 0, pl.ds(at + level, 1), :], (ROWS, LANES))
            north = jnp.broadcast_to(ns[kind, 1, pl.ds(at + level, 1), :], (ROWS, LANES))
            return (
                jnp.where(row == 0, south, pltpu.roll(x, 1, axis=0)),
                jnp.where(row == ROWS - 1, north, pltpu.roll(x, ROWS - 1, axis=0)),
            )

        H, U, V = (traj[f, j] for f in range(3))
        p, q, r = (mu[f, j] for f in range(3))
        H_w, H_e = east_west(H, ewt, level)
        U_w, U_e = east_west(U, ewt, LEV + level)
        p_w, p_e = east_west(p, ewm, level)
        q_w, q_e = east_west(q, ewm, LEV + level)
        H_s, H_n = south_north(H, 0, 0)
        V_s, V_n = south_north(V, 0, LEV)
        p_s, p_n = south_north(p, 1, 0)
        r_s, r_n = south_north(r, 1, LEV)
        gx_e, gx_w = (0.25 * cx) * (p_e - p), (0.25 * cx) * (p - p_w)
        gy_n = jnp.where(no_north, 0.0, (0.25 * cy) * (p_n - p))
        gy_s = jnp.where(no_south, 0.0, (0.25 * cy) * (p - p_s))
        out[0, j] = (
            p + ((U + U_e) * gx_e + (U_w + U) * gx_w) + ((V + V_n) * gy_n + (V_s + V) * gy_s)
            + cg * ((q_e - q_w) + (r_n - r_s))
        )
        out[1, j] = q + ca * (U_e * q_e - U_w * q_w) + ((H + H_e) * gx_e + (H_w + H) * gx_w)
        out[2, j] = r + ca * (V_n * r_n - V_s * r_s) + ((H + H_n) * gy_n + (H_s + H) * gy_s)
        return unused

    lax.fori_loop(0, LEVELS_STEP, level_step, 0)


TABLES, INVERSE_K2 = tables()


def per_device(trajectory, adjoint_in, cutoffs):
    f32 = jnp.float32
    whole = pl.BlockSpec(memory_space=pltpu.VMEM)
    anywhere = pl.BlockSpec(memory_space=pl.ANY)
    slots = pltpu.VMEM((SLOTS, 16, HALF, LANES), f32)
    dma = pltpu.SemaphoreType.DMA
    mu, ewt, ewm, ns = pl.pallas_call(
        exchange_kernel,
        out_shape=(
            jax.ShapeDtypeStruct((PAIRS, ROWS, LANES), f32),
            jax.ShapeDtypeStruct((2, ROWS, LANES), f32),
            jax.ShapeDtypeStruct((2, ROWS, LANES), f32),
            jax.ShapeDtypeStruct((2, 2, 2 * LEV, LANES), f32),
        ),
        in_specs=[anywhere, anywhere, whole, whole, anywhere],
        out_specs=(anywhere, whole, whole, whole),
        scratch_shapes=[
            pltpu.VMEM((PAIRS, ROWS, LANES), f32),
            pltpu.VMEM((PAIRS, ROWS, LANES), f32),
            slots, slots, slots, slots,
            pltpu.VMEM((2, 2, 8, 256, 256), jnp.bfloat16),
            pltpu.VMEM((2, 8, ROWS, 256), f32),
            pltpu.VMEM((2, 2, ROWS, LANES), f32),
            pltpu.VMEM((2, 2, ROWS, LANES), f32),
            pltpu.VMEM((2, 2, 2 * LEV, LANES), f32),
            pltpu.VMEM((2, 2, 2 * LEV, LANES), f32),
            dma((SLOTS,)), dma((CHUNKS,)), dma((SLOTS,)), dma((SLOTS,)), dma((SLOTS,)), dma((SLOTS,)),
            dma((SLOTS,)), dma((CHUNKS,)),
            dma((2, 2)), dma((2, 2)), dma((2, 2)), dma((2, 2)), dma((4,)),
        ],
        compiler_params=pltpu.CompilerParams(
            collective_id=0, has_side_effects=True, vmem_limit_bytes=48 << 20
        ),
        name="exchange_filter",
    )(
        adjoint_in.reshape(PAIRS, ROWS, LANES),
        trajectory.reshape(PAIRS, ROWS, LANES),
        cutoffs,
        jnp.asarray(INVERSE_K2),
        jnp.asarray(TABLES),
    )
    field = pl.BlockSpec((3, LEVELS_STEP, ROWS, LANES), lambda i: (0, i, 0, 0))
    return pl.pallas_call(
        stencil_kernel,
        grid=(LEV // LEVELS_STEP,),
        out_shape=jax.ShapeDtypeStruct((3, LEV, ROWS, LANES), f32),
        in_specs=[field, field, whole, whole, whole],
        out_specs=field,
        compiler_params=pltpu.CompilerParams(vmem_limit_bytes=24 << 20),
        name="adjoint_stencil",
    )(trajectory, mu.reshape(3, LEV, ROWS, LANES), ewt, ewm, ns)


def solution(mesh):
    in_specs = (P(None, None, "lat", "lon"), P(None, None, "lat", "lon"), P())
    out_specs = P(None, None, "lat", "lon")
    return jax.shard_map(
        per_device, mesh=mesh, in_specs=in_specs, out_specs=out_specs, check_vma=False
    )
```

time: 467 us -> 71.5 us (0.15)
  matrix products: 234 us -> 0 us
  waiting for transfers between devices: 73.7 us -> 0 us
  Pallas kernels: 0 us -> 69.6 us
  other arithmetic: 61.6 us -> 0 us
  local copies, waits for them, and re-layouts: 57.1 us -> 1.38 us
  starting transfers between devices: 28.6 us -> 0 us
  loops' own time: 11.6 us -> 0 us
    dot_general x8 -> x0, matrix products: 234 us -> none  [the longest x4 123 us: add_block(): spectrum = jnp.dot(rows, table, precision=lax.Precision.HIGHEST)]
    pallas_call x0 -> x2, Pallas kernels: none -> 69.6 us  [the longest x1 59.9 us: per_device(): pl.pallas_call(exchange_kernel, out_shape=(jax.ShapeDtypeStruct((PAIRS, R...]
    all_to_all x2 -> x0, waiting for transfers between devices: 41.8 us -> none  [the longest x1 41.8 us: per_device(): lax.all_to_all(flat, 'lon', split_axis=0, concat_axis=1, tiled=True)]
    ppermute x8 -> x0, waiting for transfers between devices: 31.9 us -> none  [the longest x4 31.9 us: padded(): before = lax.ppermute(last, axis, up)]
    broadcast_in_dim x3 -> x0, other arithmetic: 22.2 us -> none  [the longest x2 22.2 us: out_region(): h_in, u_in, v_in = (delta[0], delta[1], delta[2])]
    ppermute x8 -> x0, starting transfers between devices: 16.2 us -> none  [the longest x4 8.9 us: padded(): before = lax.ppermute(last, axis, up)]
    slice x4 -> x0, local copies, waits for them, and re-layouts: 13.7 us -> none  [the longest x3 10.6 us: padded(): last = lax.slice_in_dim(array, length - width, length, axis=dim)]
    all_to_all x2 -> x0, starting transfers between devices: 12.4 us -> none  [the longest x1 7.3 us: per_device(): lax.all_to_all(flat, 'lon', split_axis=0, concat_axis=1, tiled=True)]
  transfers between devices with their start and end apart: 10 -> 0, of which waited for: 2 -> 0; matrix products, arithmetic and copies ran while one was open for 10% -> 0% of each run, Pallas kernels for 0% -> 0%
where the time goes in v1:
time: 71.5 us; the launch traced here: 71 us
  Pallas kernels  69.6 us (97%)
  local copies, waits for them, and re-layouts  1.38 us (2%)
    pallas_call x1, Pallas kernels, per_device(): pl.pallas_call(exchange_kernel, out_shape=(jax.ShapeDtypeStruct((PAIRS, R...  59.9 us
    pallas_call x1, Pallas kernels, per_device(): pl.pallas_call(stencil_kernel, grid=(LEV // LEVELS_STEP,), out_shape=jax....  9.68 us

profile of v1, /device:TPU:1, one launch (start us, length us, event | category | flops | bytes accessed | tf_op | source)
XLA Modules:
  0.0 71.0 jit_solution(10281363617556804614)
XLA Ops:
  0.0 0.0 copy-start.1
  0.0 0.7 copy-done.1
  0.7 0.0 copy-start.2
  0.7 0.7 copy-done.2
  1.4 0.0 copy-start
  1.4 59.9 %exchange_filter.1 = (f32[96,64,128]{2,1,0:T(8,128)S(1)}, f32[2,64,128]{2,1,0:T(8,128)S(1)}, f32[2,64,128]{2,1,0:T(8,128)S(1)}, f32[2,2,64,128]{3,2,1,0:T(8,128)S(1)}) custom-call(f32[96,64,128]{2,1,0:T(8,128)} %bitcast.5, f32[96,64,128]{2,1,0:T(8,128)} %bitcast.3, s32[2,64]{1,0:T(2,128)S(1)} %copy-done.2, f32[8,256]{1,0:T(8,128)S(1)} %copy-done.1, ...), custom_call_target="tpu_custom_call" | custom-call | tf_op jit(solution)/shard_map/exchange_filter/pallas_call | solution.py:471
  61.3 0.0 copy-done
  61.3 9.7 %adjoint_stencil.1 = f32[3,32,64,128]{3,2,1,0:T(8,128)} custom-call(f32[3,32,64,128]{3,2,1,0:T(8,128)S(1)} %copy-done, f32[3,32,64,128]{3,2,1,0:T(8,128)S(1)} %bitcast.4, f32[2,64,128]{2,1,0:T(8,128)S(1)} %get-tuple-element.10.ewt, f32[2,64,128]{2,1,0:T(8,128)S(1)} %get-tuple-element.11.ewm, f32[2,2,64,128]{3,2,1,0:T(8,128)S(1)} %get-tuple-element.12.ns), custom_call_target="tpu_custom_call" | custom-call | tf_op jit(solution)/shard_map/adjoint_stencil/pallas_call | solution.py:507
Async XLA Ops:
  0.0 0.7 copy-start.1
  0.7 0.7 copy-start.2
  1.4 59.9 %copy-start = (f32[3,32,64,128]{3,2,1,0:T(8,128)S(1)}, f32[3,32,64,128]{3,2,1,0:T(8,128)}, u32[]{:S(2)}) copy-start(f32[3,32,64,128]{3,2,1,0:T(8,128)} %traj.1) | copy-start | bytes 9437188

commit v2 on v1

v2 whole, which is shorter than its diff:
```python
import functools

import jax
import jax.numpy as jnp
import ml_dtypes
import numpy as np
from jax import lax
from jax.experimental import pallas as pl
from jax.experimental.pallas import tpu as pltpu
from jax.sharding import PartitionSpec as P

MESH = pl.DeviceIdType.MESH
NLON, LEV, ROWS, LANES, LON, LAT = 2048, 32, 64, 128, 16, 8
PAIRS = 3 * LEV
GROUP, HALF, CHUNKS = 8, 32, 24
HOME, SINGLE, NEAR, FAR = (7, 4), (3, 2), (3, 1), (3, 1)
LAG = 2
SLOTS = max(sum(HOME), sum(SINGLE), 2 * sum(NEAR))
cx, cy, cg, ca = 0.25, 0.25, 0.3, 0.25


def tables():
    m = np.arange(LANES)[:, None]
    k = np.arange(LANES)[None, :]
    forward = np.zeros((8, 256, 256))
    inverse = np.zeros((8, 256, 256))
    wave = np.zeros((8, 256))

    def angle(freq):
        return 2.0 * np.pi / NLON * ((freq * m) % NLON)

    for q in range(1, 8):
        freq = 16 * k + q
        cos, sin = np.cos(angle(freq)), np.sin(angle(freq))
        forward[q] = np.block([[cos, -sin], [sin, cos]])
        inverse[q] = forward[q].T / NLON
        wave[q] = np.tile(np.minimum(freq, NLON - freq)[0], 2)
    index = np.arange(LANES)
    for at, q, is_cos, order in (
        (0, 0, index <= 64, np.where(index <= 64, index, index - 64)),
        (128, 8, index < 64, index % 64),
    ):
        freq = (16 * order + q)[None, :]
        block = np.where(is_cos[None, :], np.cos(angle(freq)), -np.sin(angle(freq)))
        weight = np.where((freq == 0) | (freq == NLON // 2), 1.0, 2.0)
        forward[0, at : at + 128, at : at + 128] = block
        inverse[0, at : at + 128, at : at + 128] = (block * weight).T / NLON
        wave[0, at : at + 128] = freq[0]
    both = np.stack([forward, inverse])
    high = both.astype(np.float32).astype(ml_dtypes.bfloat16)
    low = (both - high.astype(np.float64)).astype(np.float32).astype(ml_dtypes.bfloat16)
    damp = (1.0 / np.maximum(wave, 1.0) ** 2).astype(np.float32)
    return np.stack([high, low], 1), damp


def cadd(a, b, sign=1.0):
    re = a[0] + b[0] if sign > 0 else a[0] - b[0]
    if a[1] is None and b[1] is None:
        return (re, None)
    if a[1] is None:
        return (re, b[1] if sign > 0 else -b[1])
    if b[1] is None:
        return (re, a[1])
    return (re, a[1] + b[1] if sign > 0 else a[1] - b[1])


def conj(a):
    return a if a[1] is None else (a[0], -a[1])


def ctwist(a, k, n, sign):
    if k == 0:
        return a
    re, im = a
    if 4 * k == n:
        if im is None:
            return (jnp.zeros_like(re), re if sign > 0 else -re)
        return (-im, re) if sign > 0 else (im, -re)
    c, s = float(np.cos(2 * np.pi * k / n)), sign * float(np.sin(2 * np.pi * k / n))
    if im is None:
        return (re * c, re * s)
    if 8 * k == n:
        return ((re - im) * c, (re + im) * c) if sign > 0 else ((re + im) * c, (im - re) * c)
    return (re * c - im * s, re * s + im * c)


def real_dft(xs):
    n = len(xs)
    if n == 1:
        return [(xs[0], None)]
    if n == 2:
        return [(xs[0] + xs[1], None), (xs[0] - xs[1], None)]
    even, odd = real_dft(xs[0::2]), real_dft(xs[1::2])
    out = [None] * (n // 2 + 1)
    for k in range(n // 4 + 1):
        turned = ctwist(odd[k], k, n, -1)
        out[k] = cadd(even[k], turned)
        if k != n // 4:
            out[n // 2 - k] = conj(cadd(even[k], turned, -1.0))
    return out


def real_inverse(spec):
    n = 2 * (len(spec) - 1)
    if n == 2:
        return [spec[0][0] + spec[1][0], spec[0][0] - spec[1][0]]
    even, odd = [], []
    for k in range(n // 4 + 1):
        other = conj(spec[n // 2 - k])
        even.append(cadd(spec[k], other))
        odd.append(ctwist(cadd(spec[k], other, -1.0), k, n, 1))
    for part in (even, odd):
        part[0] = (part[0][0], None)
        part[-1] = (part[-1][0], None)
    a, b = real_inverse(even), real_inverse(odd)
    return [v for both in zip(a, b) for v in both]


def product(z, high, low):
    hi = z.astype(jnp.bfloat16)
    lo = (z - hi.astype(jnp.float32)).astype(jnp.bfloat16)
    rows = z.shape[0]
    main = jnp.dot(jnp.concatenate([hi, lo], 0), high, preferred_element_type=jnp.float32)
    rest = jnp.dot(hi, low, preferred_element_type=jnp.float32)
    return main[:rows] + main[rows:] + rest


def filter_chunk(blocks, table, damp_of):
    spec = real_dft(blocks)
    groups = [jnp.concatenate([spec[0][0], spec[8][0]], 1)]
    groups += [jnp.concatenate(spec[q], 1) for q in range(1, 8)]
    back = []
    for q in range(8):
        waves = product(groups[q], table[0, 0, q], table[0, 1, q]) * damp_of(q)
        back.append(product(waves, table[1, 0, q], table[1, 1, q]))
    spec = [(back[0][:, :LANES], None)]
    spec += [(back[q][:, :LANES], back[q][:, LANES:]) for q in range(1, 8)]
    spec += [(back[0][:, LANES:], None)]
    return real_inverse(spec)


def flip_bits(value, mask, width=4):
    out = 0
    for bit in range(width):
        own = (value // (1 << bit)) % 2
        out = out + (1 << bit) * ((1 - own) if (mask >> bit) & 1 else own)
    return out


def numbered(kind, index, side):
    kinds = (HOME, SINGLE, NEAR, FAR)
    early, late = kinds[kind]
    first = sum(k[0] for k in kinds[:kind])
    beside = sum(k[1] - 1 for k in kinds[:kind])
    base = 2 * CHUNKS // 3
    last = base + 2 * kind + side
    before = base + 2 * (beside + index - early) + 1 - side
    return jnp.where(index < early, first + index, jnp.where(index == early + late - 1, last, before))


def exchange_kernel(
    adj, traj, cuts_in, inverse_k2_in, table_in,
    mu_out, ew_out, ns_out,
    mu, trj, rin, rcv, yout, table, damp, cuts, inverse_k2, ew_send, ew_recv, ns_send, ns_recv,
    rin_sem, relay_sem, fs_sem, rcv_sem, bs_sem, ro_sem, mu_sem,
    ews_sem, ewr_sem, nss_sem, nsr_sem, local_sem,
):
    lon = lax.axis_index("lon")
    lat = lax.axis_index("lat")
    core, chip = lon % 2, lon // 2
    mirror = flip_bits(lon, 8)
    own_side = jnp.where(lat < LAT // 2, 0, 1)
    is_cap = (lat == 0) | (lat == LAT - 1)
    is_single = (lat == 2) | (lat == 5)
    is_double = (lat == 1) | (lat == 6)
    helps = is_single | is_double
    lower = lat < LAT // 2
    waves = jnp.where(is_cap, sum(HOME), jnp.where(is_single, sum(SINGLE), jnp.where(is_double, sum(NEAR), 0)))
    width = jnp.where(is_double, 2, 1)
    lead, lag = jnp.where(is_cap, 0, 1), jnp.where(is_cap, 0, LAG)

    def to(lon_at, lat_at):
        return {"lon": lon_at, "lat": lat_at}

    peers = [to(flip_bits(lon, k), lat) for k in range(1, 16)]
    peers += [to(lon, (lat + k) % LAT) for k in (1, 2, 6, 7)]
    peers += [to(mirror, flip_bits(lat, 1, 3))]
    barrier = pltpu.get_barrier_semaphore()
    for peer in peers:
        pl.semaphore_signal(barrier, inc=1, device_id=peer, device_id_type=MESH)

    traj_copy = pltpu.make_async_copy(traj, trj, local_sem.at[1])
    mu_copy = pltpu.make_async_copy(adj, mu.at[pl.ds(0, PAIRS)], local_sem.at[2])
    small_copies = [
        pltpu.make_async_copy(cuts_in, cuts, local_sem.at[3]),
        pltpu.make_async_copy(inverse_k2_in, inverse_k2, local_sem.at[4]),
        pltpu.make_async_copy(table_in, table, local_sem.at[0]),
    ]

    def chunk_of(ref, chunk):
        pair = pl.multiple_of(GROUP * (chunk // 2), GROUP)
        row = pl.multiple_of(HALF * (chunk % 2), HALF)
        return ref.at[pl.ds(pair, GROUP), pl.ds(row, HALF)]

    @pl.when(is_cap)
    def _():
        for s in range(sum(HOME)):
            pltpu.make_async_copy(chunk_of(adj, numbered(0, s, own_side)), rin.at[s], rin_sem.at[s]).start()

    traj_copy.start()
    for copy in small_copies:
        copy.start()

    @pl.when(jnp.logical_not(is_cap))
    def _():
        mu_copy.start()

    pl.semaphore_wait(barrier, len(peers))

    def relay(chunk, device, slot):
        pltpu.make_async_remote_copy(
            src_ref=chunk_of(adj, chunk), dst_ref=rin.at[slot],
            send_sem=relay_sem.at[chunk], recv_sem=rin_sem.at[slot],
            device_id=device, device_id_type=MESH,
        ).start()

    def step_of(s):
        odd = s % 2
        far = is_double & (odd == 1)
        side = jnp.where(far, 1 - own_side, own_side)
        double = jnp.where(odd == 1, numbered(3, s // 2, side), numbered(2, s // 2, side))
        chunk = jnp.where(is_cap, numbered(0, s, side), jnp.where(is_single, numbered(1, s, side), double))
        flip = jnp.where(is_double & (odd == 0), 1, 0)
        return side, chunk, flip

    def home_lon(member, flip):
        return jnp.where(flip == 1, (member + 8) % 16, member)

    def landing(s):
        unused_side, chunk, unused_flip = step_of(s)
        return jnp.where(is_cap, chunk, 2 * PAIRS // GROUP + s)

    def remote(src, dst, send_sem, recv_sem, member):
        pltpu.make_async_remote_copy(
            src_ref=src, dst_ref=dst, send_sem=send_sem, recv_sem=recv_sem,
            device_id=to(member, lat), device_id_type=MESH,
        ).start()

    def forward(s):
        unused_side, unused_chunk, flip = step_of(s)
        pltpu.make_async_copy(rin.at[s], rin.at[s], rin_sem.at[s]).wait()
        dst = rcv.at[s, home_lon(lon, flip)]
        for k in range(1, 8):
            owner = flip_bits(chip, k, 3)
            remote(rin.at[s, owner], dst, fs_sem.at[s], rcv_sem.at[s], 2 * owner + s % 2)

        @pl.when(core == s % 2)
        def _():
            pltpu.make_async_copy(rin.at[s, chip], dst, rcv_sem.at[s]).start()

        @pl.when(core != s % 2)
        def _():
            remote(rin.at[s, chip], dst, fs_sem.at[s], rcv_sem.at[s], 2 * chip + 1 - core)

    def work(s):
        side, chunk, flip = step_of(s)
        row = pl.multiple_of(HALF * (chunk % 2), HALF)
        pltpu.make_async_copy(rcv.at[s], rcv.at[s], rcv_sem.at[s]).wait()
        done = filter_chunk(
            [rcv[s, d] for d in range(16)], table, lambda q: damp[side, q, pl.ds(row, HALF), :]
        )
        for d in range(16):
            yout[s, d] = done[d]
        land = landing(s)
        pair = GROUP * (land // 2) + chip
        dst = mu.at[pair, pl.ds(pl.multiple_of(HALF * (land % 2), HALF), HALF)]
        for k in range(1, 16):
            member = flip_bits(lon, k)
            remote(yout.at[s, home_lon(member, flip)], dst, bs_sem.at[s], mu_sem.at[land], member)
        pltpu.make_async_copy(yout.at[s, home_lon(lon, flip)], dst, mu_sem.at[land]).start()

    def deliver(s):
        side, chunk, flip = step_of(s)
        part = chunk_of(mu, landing(s))
        pltpu.make_async_copy(part, part, mu_sem.at[landing(s)]).wait()
        pltpu.make_async_remote_copy(
            src_ref=part, dst_ref=chunk_of(mu, chunk), send_sem=ro_sem.at[s], recv_sem=mu_sem.at[chunk],
            device_id=to(home_lon(lon, flip), (LAT - 1) * side), device_id_type=MESH,
        ).start()

    @pl.when(is_cap)
    def _():
        turn = jnp.where(lower, 2, LAT - 2)
        single, other = (lat + turn) % LAT, (lat + LAT - turn) % LAT
        outer = to(mirror, flip_bits(lat, 1, 3))
        for s in range(max(sum(SINGLE), sum(NEAR))):
            if s < sum(NEAR):
                relay(numbered(2, s, own_side), outer, 2 * s)
                relay(numbered(3, s, own_side), to(lon, other), 2 * s + 1)
            if s < sum(SINGLE):
                relay(numbered(1, s, own_side), to(lon, single), s)

        @pl.loop(0, sum(HOME))
        def _(s):
            forward(s)

    lane = lax.broadcasted_iota(jnp.int32, (ROWS, LANES), 1)

    def pack(ref, kind):
        def body(level, packed):
            for at, f in ((0, 0), (LANES // 2, 1)):
                target = at + 2 * level
                turned = pltpu.roll(ref[f * LEV + level], target, axis=1)
                packed = jnp.where((lane == target) | (lane == (target + LANES - 1) % LANES), turned, packed)
            return packed

        ew_send[kind] = lax.fori_loop(0, LEV, body, jnp.zeros((ROWS, LANES), jnp.float32))

    def pack_rows(ref, kind, side):
        at = (0, ROWS - 1)[side]
        for first, f in ((0, 0), (LEV, 2)):
            @pl.loop(0, LEV)
            def _(level):
                ns_send[kind, side, pl.ds(first + level, 1), :] = ref[f * LEV + level, at : at + 1, :]

    def ew_copies(kind):
        return [
            pltpu.make_async_remote_copy(
                src_ref=ew_send.at[kind], dst_ref=ew_recv.at[kind, 1 - side],
                send_sem=ews_sem.at[kind, side], recv_sem=ewr_sem.at[kind, 1 - side],
                device_id=to((lon + step) % LON, lat), device_id_type=MESH,
            )
            for side, step in ((0, LON - 1), (1, 1))
        ]

    def ns_copies(kind):
        return [
            pltpu.make_async_remote_copy(
                src_ref=ns_send.at[kind, side], dst_ref=ns_recv.at[kind, 1 - side],
                send_sem=nss_sem.at[kind, side], recv_sem=nsr_sem.at[kind, 1 - side],
                device_id=to(lon, (lat + step) % LAT), device_id_type=MESH,
            )
            for side, step in ((0, LAT - 1), (1, 1))
        ]

    inner = (lat > 0, lat < LAT - 1)

    def send_columns(ref, kind):
        pack(ref, kind)
        for copy in ew_copies(kind):
            copy.start()

    def send_rows(ref, kind):
        for side, copy in enumerate(ns_copies(kind)):
            @pl.when(inner[side])
            def _():
                pack_rows(ref, kind, side)
                copy.start()

    traj_copy.wait()
    send_columns(trj, 0)
    send_rows(trj, 0)

    @pl.when(jnp.logical_not(is_cap))
    def _():
        mu_copy.wait()
        send_columns(mu, 1)
        send_rows(mu, 1)

    row_at = lax.broadcasted_iota(jnp.int32, (ROWS, ROWS), 0)
    col_at = lax.broadcasted_iota(jnp.int32, (ROWS, ROWS), 1)
    for copy in small_copies:
        copy.wait()
    for side in range(2):
        cut = cuts[side : side + 1, :].astype(jnp.float32)
        column = jnp.sum(jnp.where(row_at == col_at, cut, 0.0), axis=1, keepdims=True)
        for q in range(8):
            damp[side, q] = jnp.minimum(1.0, column * column * inverse_k2[q : q + 1, :])

    @pl.loop(0, jnp.where(waves > 0, waves + lag, 0))
    def _(t):
        for j in range(2):
            @pl.when(helps & (t < waves) & (j < width))
            def _():
                forward(t * width + j)

        s = jnp.where(is_double, (t - lead) * 2 + core, t - lead)

        @pl.when((t >= lead) & (t < waves + lead) & (s % 2 == core))
        def _():
            work(s)

        for j in range(2):
            @pl.when(helps & (t >= lag) & (j < width))
            def _():
                deliver((t - lag) * width + j)

    def arrived(chunk):
        part = chunk_of(mu, chunk)
        pltpu.make_async_copy(part, part, mu_sem.at[chunk]).wait()

    def out_copy(first, count, sem):
        return pltpu.make_async_copy(
            mu.at[pl.ds(first, count)], mu_out.at[pl.ds(first, count)], local_sem.at[sem]
        )

    early = 2 * CHUNKS // 3

    @pl.when(is_cap)
    def _():
        for chunk in range(early):
            arrived(chunk)
        send_columns(mu, 1)
        for group in range(CHUNKS // 6):
            arrived(early + 2 * group + 1 - own_side)
        send_rows(mu, 1)

    out_copy(0, 2 * LEV, 5).start()

    for kind in range(2):
        for copy in ew_copies(kind):
            copy.wait()
    even = lane % 2 == 0
    first_part = (lane < LANES // 2 - 1) | (lane == LANES - 1)

    def swapped(x):
        return pltpu.roll(x, LANES // 2, axis=1)

    def beyond(kind):
        return jnp.where(
            even, pltpu.roll(ew_recv[kind, 0], 1, axis=1), pltpu.roll(ew_recv[kind, 1], LANES - 1, axis=1)
        )

    state, state_out = ew_send[0], beyond(0)
    adjoint, adjoint_out = ew_send[1], beyond(1)
    p_in = jnp.where(first_part, adjoint, swapped(adjoint))
    p_out = jnp.where(first_part, adjoint_out, swapped(adjoint_out))
    q_out = jnp.where(first_part, swapped(adjoint_out), adjoint_out)
    term = (0.25 * cx) * (swapped(state) + swapped(state_out)) * (p_out - p_in)
    term = term + jnp.where(first_part, cg, ca * state_out) * q_out
    ew_out[...] = jnp.where(even, -term, term)

    for side in range(2):
        @pl.when(inner[side])
        def _():
            for kind in range(2):
                ns_copies(kind)[side].wait_send()
                whole = ns_recv.at[kind, side]
                pltpu.make_async_copy(whole, whole, nsr_sem.at[kind, side]).wait()
            H_in, V_in = ns_send[0, side, :LEV], ns_send[0, side, LEV:]
            H_out, V_out = ns_recv[0, side, :LEV], ns_recv[0, side, LEV:]
            p_diff = (0.25 * cy) * (ns_recv[1, side, :LEV] - ns_send[1, side, :LEV])
            r_out = ns_recv[1, side, LEV:]
            sign = 1.0 if side else -1.0
            ns_out[side, :LEV] = sign * ((V_in + V_out) * p_diff + cg * r_out)
            ns_out[side, LEV:] = sign * ((H_in + H_out) * p_diff + ca * V_out * r_out)

        @pl.when(jnp.logical_not(inner[side]))
        def _():
            ns_out[side] = jnp.zeros((2 * LEV, LANES), jnp.float32)

    @pl.when(is_cap)
    def _():
        for group in range(CHUNKS // 6):
            arrived(early + 2 * group + own_side)

    out_copy(2 * LEV, LEV, 6).start()

    @pl.when(is_cap)
    def _():
        for kind in (1, 2, 3):
            for s in range(sum((HOME, SINGLE, NEAR, FAR)[kind])):
                chunk = numbered(kind, s, own_side)
                part = chunk_of(mu, chunk)
                pltpu.make_async_copy(part, part, relay_sem.at[chunk]).wait()

    @pl.loop(0, waves * width)
    def _(s):
        most = rin.at[s, pl.ds(0, 7)]

        @pl.when(core == s % 2)
        def _():
            pltpu.make_async_copy(most, most, fs_sem.at[s]).wait()
            sent = rcv.at[s, pl.ds(0, 15)]
            pltpu.make_async_copy(sent, sent, bs_sem.at[s]).wait()

        @pl.when(core != s % 2)
        def _():
            pltpu.make_async_copy(rin.at[s], rin.at[s], fs_sem.at[s]).wait()

        @pl.when(helps)
        def _():
            pltpu.make_async_copy(rin.at[s], rin.at[s], ro_sem.at[s]).wait()

    out_copy(0, 2 * LEV, 5).wait()
    out_copy(2 * LEV, LEV, 6).wait()


LEVELS_STEP = 8


def stencil_kernel(traj, mu, ew, ns, out):
    first = pl.program_id(0) * LEVELS_STEP
    row = lax.broadcasted_iota(jnp.int32, (ROWS, LANES), 0)
    lane = lax.broadcasted_iota(jnp.int32, (ROWS, LANES), 1)
    edge = (lane == 0) | (lane == LANES - 1)

    def fluxes(p, a, b, r, axis):
        size = (ROWS, LANES)[axis]
        last = (row, lane)[axis] == size - 1

        def after(x):
            return pltpu.roll(x, size - 1, axis=axis)

        a_after = after(a)
        slope = jnp.where(last, 0.0, (0.25 * cx) * (after(p) - p))
        r_after = jnp.where(last, 0.0, after(r))
        r_here = jnp.where(last, 0.0, r)
        flux_h = (a + a_after) * slope
        flux_r = (b + after(b)) * slope
        to_h = (flux_h + cg * r_after) + pltpu.roll(flux_h - cg * r_here, 1, axis=axis)
        to_r = (flux_r + ca * (a_after * r_after)) + pltpu.roll(flux_r - ca * (a * r_here), 1, axis=axis)
        return to_h, to_r

    for j in range(LEVELS_STEP):
        level = first + j
        H, U, V = (traj[f, j] for f in range(3))
        p, q, r = (mu[f, j] for f in range(3))
        x_h, x_u = fluxes(p, U, H, q, 1)
        y_h, y_v = fluxes(p, V, H, r, 0)
        over_h = jnp.where(edge, pltpu.roll(ew[...], (LANES - 2 * level) % LANES, axis=1), 0.0)
        over_u = jnp.where(edge, pltpu.roll(ew[...], (LANES + LANES // 2 - 2 * level) % LANES, axis=1), 0.0)
        out[0, j] = p + x_h + y_h + over_h
        out[1, j] = q + x_u + over_u
        out[2, j] = r + y_v
        for side, at in ((0, 0), (1, ROWS - 1)):
            out[0, j, at : at + 1, :] += ns[side, pl.ds(level, 1), :]
            out[2, j, at : at + 1, :] += ns[side, pl.ds(LEV + level, 1), :]


TABLES, INVERSE_K2 = tables()


def per_device(trajectory, adjoint_in, cutoffs):
    f32 = jnp.float32
    whole = pl.BlockSpec(memory_space=pltpu.VMEM)
    anywhere = pl.BlockSpec(memory_space=pl.ANY)
    vmem = pltpu.VMEM
    dma = pltpu.SemaphoreType.DMA
    extra = GROUP * ((2 * sum(NEAR) + 1) // 2)
    if sum(SINGLE) > 2 * sum(NEAR):
        extra = GROUP * ((sum(SINGLE) + 1) // 2)
    mu, ew, ns = pl.pallas_call(
        exchange_kernel,
        out_shape=(
            jax.ShapeDtypeStruct((PAIRS, ROWS, LANES), f32),
            jax.ShapeDtypeStruct((ROWS, LANES), f32),
            jax.ShapeDtypeStruct((2, 2 * LEV, LANES), f32),
        ),
        in_specs=[anywhere] * 5,
        out_specs=(anywhere, whole, whole),
        scratch_shapes=[
            vmem((PAIRS + extra, ROWS, LANES), f32),
            vmem((PAIRS, ROWS, LANES), f32),
            vmem((SLOTS, GROUP, HALF, LANES), f32),
            vmem((SLOTS, 16, HALF, LANES), f32),
            vmem((SLOTS, 16, HALF, LANES), f32),
            vmem((2, 2, 8, 256, 256), jnp.bfloat16),
            vmem((2, 8, ROWS, 256), f32),
            vmem((2, ROWS), jnp.int32),
            vmem((8, 256), f32),
            vmem((2, ROWS, LANES), f32),
            vmem((2, 2, ROWS, LANES), f32),
            vmem((2, 2, 2 * LEV, LANES), f32),
            vmem((2, 2, 2 * LEV, LANES), f32),
            dma((SLOTS,)), dma((CHUNKS,)), dma((SLOTS,)), dma((SLOTS,)), dma((SLOTS,)), dma((SLOTS,)),
            dma((CHUNKS + SLOTS,)),
            dma((2, 2)), dma((2, 2)), dma((2, 2)), dma((2, 2)), dma((7,)),
        ],
        compiler_params=pltpu.CompilerParams(
            collective_id=0, has_side_effects=True, vmem_limit_bytes=48 << 20
        ),
        name="exchange_filter",
    )(
        adjoint_in.reshape(PAIRS, ROWS, LANES),
        trajectory.reshape(PAIRS, ROWS, LANES),
        cutoffs,
        jnp.asarray(INVERSE_K2),
        jnp.asarray(TABLES),
    )
    field = pl.BlockSpec((3, LEVELS_STEP, ROWS, LANES), lambda i: (0, i, 0, 0))
    return pl.pallas_call(
        stencil_kernel,
        grid=(LEV // LEVELS_STEP,),
        out_shape=jax.ShapeDtypeStruct((3, LEV, ROWS, LANES), f32),
        in_specs=[field, field, whole, whole],
        out_specs=field,
        compiler_params=pltpu.CompilerParams(vmem_limit_bytes=24 << 20),
        name="adjoint_stencil",
    )(trajectory, mu.reshape(3, LEV, ROWS, LANES), ew, ns)


def solution(mesh):
    in_specs = (P(None, None, "lat", "lon"), P(None, None, "lat", "lon"), P())
    out_specs = P(None, None, "lat", "lon")
    return jax.shard_map(
        per_device, mesh=mesh, in_specs=in_specs, out_specs=out_specs, check_vma=False
    )
```

time: 71.5 us -> 57.8 us (0.81)
  Pallas kernels: 69.6 us -> 56.2 us
    pallas_call x1, Pallas kernels: 59.9 us -> 50.7 us  [per_device(): pl.pallas_call(exchange_kernel, out_shape=(jax.ShapeDtypeStruct((PAIRS, R...]
    pallas_call x1, Pallas kernels: 9.68 us -> 5.56 us  [per_device(): pl.pallas_call(stencil_kernel, grid=(LEV // LEVELS_STEP,), out_shape=jax....]
where the time goes in v2:
time: 57.8 us; the launch traced here: 57.6 us
  Pallas kernels  56.2 us (97%)
  local copies, waits for them, and re-layouts  1.38 us (2%)
    pallas_call x1, Pallas kernels, per_device(): pl.pallas_call(exchange_kernel, out_shape=(jax.ShapeDtypeStruct((PAIRS, R...  50.7 us
    pallas_call x1, Pallas kernels, per_device(): pl.pallas_call(stencil_kernel, grid=(LEV // LEVELS_STEP,), out_shape=jax....  5.56 us
    unnamed x6, local copies, waits for them, and re-layouts  1.38 us

profile of v2, /device:TPU:1, one launch (start us, length us, event | category | flops | bytes accessed | tf_op | source)
XLA Modules:
  0.0 57.6 jit_solution(4716613601600120871)
XLA Ops:
  0.0 0.0 copy-start.1
  0.0 0.7 %copy-done.1 = f32[8,256]{1,0:T(8,128)S(1)} copy-done((f32[8,256]{1,0:T(8,128)S(1)}, f32[8,256]{1,0:T(8,128)}, u32[]{:S(2)}) %copy-start.1) | copy-done | bytes 8216
  0.7 0.0 copy-start.2
  0.7 0.7 %copy-done.2 = s32[2,64]{1,0:T(2,128)S(1)} copy-done((s32[2,64]{1,0:T(2,128)S(1)}, s32[2,64]{1,0:T(2,128)}, u32[]{:S(2)}) %copy-start.2) | copy-done | bytes 536
  1.4 0.0 copy-start
  1.4 50.7 %exchange_filter.1 = (f32[96,64,128]{2,1,0:T(8,128)S(1)}, f32[64,128]{1,0:T(8,128)S(1)}, f32[2,64,128]{2,1,0:T(8,128)S(1)}) custom-call(f32[96,64,128]{2,1,0:T(8,128)} %bitcast.5, f32[96,64,128]{2,1,0:T(8,128)} %bitcast.3, s32[2,64]{1,0:T(2,128)S(1)} %copy-done.2, f32[8,256]{1,0:T(8,128)S(1)} %copy-done.1, bf16[2,2,8,256,256]{4,3,2,1,0:T(8,128)(2,1)} %constant.5.clone.table_in), custom_call_target="tpu_custom_call" | custom-call | tf_op jit(solution)/shard_map/exchange_filter/pallas_call | solution.py:553
  52.0 0.0 copy-done
  52.1 5.6 %adjoint_stencil.1 = f32[3,32,64,128]{3,2,1,0:T(8,128)} custom-call(f32[3,32,64,128]{3,2,1,0:T(8,128)S(1)} %copy-done, f32[3,32,64,128]{3,2,1,0:T(8,128)S(1)} %bitcast.4, f32[64,128]{1,0:T(8,128)S(1)} %get-tuple-element.9.ew, f32[2,64,128]{2,1,0:T(8,128)S(1)} %get-tuple-element.10.ns), custom_call_target="tpu_custom_call" | custom-call | tf_op jit(solution)/shard_map/adjoint_stencil/pallas_call | solution.py:592
Async XLA Ops:
  0.0 0.7 %copy-start.1 = (f32[8,256]{1,0:T(8,128)S(1)}, f32[8,256]{1,0:T(8,128)}, u32[]{:S(2)}) copy-start(f32[8,256]{1,0:T(8,128)} %constant.4.clone.inverse_k2_in) | copy-start | bytes 24580
  0.7 0.7 %copy-start.2 = (s32[2,64]{1,0:T(2,128)S(1)}, s32[2,64]{1,0:T(2,128)}, u32[]{:S(2)}) copy-start(s32[2,64]{1,0:T(2,128)} %cuts_in.1) | copy-start | bytes 1540
  1.4 50.7 %copy-start = (f32[3,32,64,128]{3,2,1,0:T(8,128)S(1)}, f32[3,32,64,128]{3,2,1,0:T(8,128)}, u32[]{:S(2)}) copy-start(f32[3,32,64,128]{3,2,1,0:T(8,128)} %traj.1) | copy-start | bytes 9437188

commit v3 on v2

--- a/solution.py
+++ b/solution.py
@@ -12,10 +12,13 @@
 MESH = pl.DeviceIdType.MESH
 NLON, LEV, ROWS, LANES, LON, LAT = 2048, 32, 64, 128, 16, 8
 PAIRS = 3 * LEV
-GROUP, HALF, CHUNKS = 8, 32, 24
-HOME, SINGLE, NEAR, FAR = (7, 4), (3, 2), (3, 1), (3, 1)
-LAG = 2
-SLOTS = max(sum(HOME), sum(SINGLE), 2 * sum(NEAR))
+GROUP, PIECE = 8, 32
+PARTS = ROWS // PIECE
+CHUNKS = PARTS * PAIRS // GROUP
+HOME, SINGLE, FAR, NEAR = (8, 1, 1), (3, 1, 1), (3, 1, 1), (2, 1, 1)
+KINDS = (HOME, SINGLE, FAR, NEAR)
+SLOTS = max(sum(kind) for kind in KINDS)
+AHEAD, LEAD, LAG = 8, 1, 2
 cx, cy, cg, ca = 0.25, 0.25, 0.3, 0.25
 
 
@@ -24,7 +27,6 @@
     k = np.arange(LANES)[None, :]
     forward = np.zeros((8, 256, 256))
     inverse = np.zeros((8, 256, 256))
-    wave = np.zeros((8, 256))
 
     def angle(freq):
         return 2.0 * np.pi / NLON * ((freq * m) % NLON)
@@ -34,7 +36,6 @@
         cos, sin = np.cos(angle(freq)), np.sin(angle(freq))
         forward[q] = np.block([[cos, -sin], [sin, cos]])
         inverse[q] = forward[q].T / NLON
-        wave[q] = np.tile(np.minimum(freq, NLON - freq)[0], 2)
     index = np.arange(LANES)
     for at, q, is_cos, order in (
         (0, 0, index <= 64, np.where(index <= 64, index, index - 64)),
@@ -45,12 +46,10 @@
         weight = np.where((freq == 0) | (freq == NLON // 2), 1.0, 2.0)
         forward[0, at : at + 128, at : at + 128] = block
         inverse[0, at : at + 128, at : at + 128] = (block * weight).T / NLON
-        wave[0, at : at + 128] = freq[0]
     both = np.stack([forward, inverse])
     high = both.astype(np.float32).astype(ml_dtypes.bfloat16)
     low = (both - high.astype(np.float64)).astype(np.float32).astype(ml_dtypes.bfloat16)
-    damp = (1.0 / np.maximum(wave, 1.0) ** 2).astype(np.float32)
-    return np.stack([high, low], 1), damp
+    return np.stack([high, low], 1)
 
 
 def cadd(a, b, sign=1.0):
@@ -148,43 +147,47 @@
 
 
 def numbered(kind, index, side):
-    kinds = (HOME, SINGLE, NEAR, FAR)
-    early, late = kinds[kind]
-    first = sum(k[0] for k in kinds[:kind])
-    beside = sum(k[1] - 1 for k in kinds[:kind])
+    plain, beside, rest = KINDS[kind]
+    plains, besides, rests = (sum(k[i] for k in KINDS[:kind]) for i in range(3))
     base = 2 * CHUNKS // 3
-    last = base + 2 * kind + side
-    before = base + 2 * (beside + index - early) + 1 - side
-    return jnp.where(index < early, first + index, jnp.where(index == early + late - 1, last, before))
+    at_beside = base + PARTS * (besides + index - plain) + (1 - side) * (PARTS - 1)
+    at = rests + index - plain - beside
+    at_rest = base + PARTS * (at // (PARTS - 1)) + at % (PARTS - 1) + side
+    return jnp.where(index < plain, plains + index, jnp.where(index < plain + beside, at_beside, at_rest))
 
 
 def exchange_kernel(
-    adj, traj, cuts_in, inverse_k2_in, table_in,
-    mu_out, ew_out, ns_out,
-    mu, trj, rin, rcv, yout, table, damp, cuts, inverse_k2, ew_send, ew_recv, ns_send, ns_recv,
-    rin_sem, relay_sem, fs_sem, rcv_sem, bs_sem, ro_sem, mu_sem,
+    adj, traj, cuts_in, table_in,
+    mu, trj, ew_out, ns_out,
+    rpass, rin, rcv, yout, table, damp, cuts, ew_send, ew_recv, ns_send, ns_recv,
+    rpass_sem, pass_sem, rin_sem, relay_sem, fs_sem, rcv_sem, bs_sem, ro_sem, mu_sem,
     ews_sem, ewr_sem, nss_sem, nsr_sem, local_sem,
 ):
     lon = lax.axis_index("lon")
     lat = lax.axis_index("lat")
     core, chip = lon % 2, lon // 2
     mirror = flip_bits(lon, 8)
-    own_side = jnp.where(lat < LAT // 2, 0, 1)
     is_cap = (lat == 0) | (lat == LAT - 1)
     is_single = (lat == 2) | (lat == 5)
-    is_double = (lat == 1) | (lat == 6)
-    helps = is_single | is_double
-    lower = lat < LAT // 2
-    waves = jnp.where(is_cap, sum(HOME), jnp.where(is_single, sum(SINGLE), jnp.where(is_double, sum(NEAR), 0)))
-    width = jnp.where(is_double, 2, 1)
-    lead, lag = jnp.where(is_cap, 0, 1), jnp.where(is_cap, 0, LAG)
+    is_far = (lat == 1) | (lat == 6)
+    is_near = (lat == 3) | (lat == 4)
+    over_y = is_single | is_far
+    helps = is_single | is_far | is_near
+    own_side = jnp.where((lat == 0) | (lat == 2) | (lat == 3) | (lat == 6), 0, 1)
+    cap_lat = (LAT - 1) * own_side
+
+    def by_kind(values):
+        helper = jnp.where(is_far, values[2], values[3])
+        return jnp.where(is_cap, values[0], jnp.where(is_single, values[1], helper))
+
+    waves = by_kind([sum(kind) for kind in KINDS])
 
     def to(lon_at, lat_at):
         return {"lon": lon_at, "lat": lat_at}
 
     peers = [to(flip_bits(lon, k), lat) for k in range(1, 16)]
-    peers += [to(lon, (lat + k) % LAT) for k in (1, 2, 6, 7)]
-    peers += [to(mirror, flip_bits(lat, 1, 3))]
+    peers += [to(lon, (lat + 1) % LAT), to(lon, (lat + LAT - 1) % LAT)]
+    peers += [to(lon, flip_bits(lat, 2, 3)), to(lon, flip_bits(lat, 6, 3)), to(mirror, flip_bits(lat, 1, 3))]
     barrier = pltpu.get_barrier_semaphore()
     for peer in peers:
         pl.semaphore_signal(barrier, inc=1, device_id=peer, device_id_type=MESH)
@@ -193,14 +196,13 @@
     mu_copy = pltpu.make_async_copy(adj, mu.at[pl.ds(0, PAIRS)], local_sem.at[2])
     small_copies = [
         pltpu.make_async_copy(cuts_in, cuts, local_sem.at[3]),
-        pltpu.make_async_copy(inverse_k2_in, inverse_k2, local_sem.at[4]),
         pltpu.make_async_copy(table_in, table, local_sem.at[0]),
     ]
 
     def chunk_of(ref, chunk):
-        pair = pl.multiple_of(GROUP * (chunk // 2), GROUP)
-        row = pl.multiple_of(HALF * (chunk % 2), HALF)
-        return ref.at[pl.ds(pair, GROUP), pl.ds(row, HALF)]
+        pair = pl.multiple_of(GROUP * (chunk // PARTS), GROUP)
+        row = pl.multiple_of(PIECE * (chunk % PARTS), PIECE)
+        return ref.at[pl.ds(pair, GROUP), pl.ds(row, PIECE)]
 
     @pl.when(is_cap)
     def _():
@@ -217,42 +219,30 @@
 
     pl.semaphore_wait(barrier, len(peers))
 
-    def relay(chunk, device, slot):
+    def relay(chunk, device, to_ref, to_sem, slot):
         pltpu.make_async_remote_copy(
-            src_ref=chunk_of(adj, chunk), dst_ref=rin.at[slot],
-            send_sem=relay_sem.at[chunk], recv_sem=rin_sem.at[slot],
+            src_ref=chunk_of(adj, chunk), dst_ref=to_ref.at[slot],
+            send_sem=relay_sem.at[chunk], recv_sem=to_sem.at[slot],
             device_id=device, device_id_type=MESH,
         ).start()
 
-    def step_of(s):
-        odd = s % 2
-        far = is_double & (odd == 1)
-        side = jnp.where(far, 1 - own_side, own_side)
-        double = jnp.where(odd == 1, numbered(3, s // 2, side), numbered(2, s // 2, side))
-        chunk = jnp.where(is_cap, numbered(0, s, side), jnp.where(is_single, numbered(1, s, side), double))
-        flip = jnp.where(is_double & (odd == 0), 1, 0)
-        return side, chunk, flip
-
-    def home_lon(member, flip):
-        return jnp.where(flip == 1, (member + 8) % 16, member)
-
-    def landing(s):
-        unused_side, chunk, unused_flip = step_of(s)
-        return jnp.where(is_cap, chunk, 2 * PAIRS // GROUP + s)
-
-    def remote(src, dst, send_sem, recv_sem, member):
+    def chunk_at(s):
+        return by_kind([numbered(kind, s, own_side) for kind in range(4)])
+
+    place = jnp.where(is_near, mirror, lon)
+
+    def remote(src, dst, send_sem, recv_sem, member, member_lat):
         pltpu.make_async_remote_copy(
             src_ref=src, dst_ref=dst, send_sem=send_sem, recv_sem=recv_sem,
-            device_id=to(member, lat), device_id_type=MESH,
+            device_id=to(member, member_lat), device_id_type=MESH,
         ).start()
 
     def forward(s):
-        unused_side, unused_chunk, flip = step_of(s)
         pltpu.make_async_copy(rin.at[s], rin.at[s], rin_sem.at[s]).wait()
-        dst = rcv.at[s, home_lon(lon, flip)]
+        dst = rcv.at[s, place]
         for k in range(1, 8):
             owner = flip_bits(chip, k, 3)
-            remote(rin.at[s, owner], dst, fs_sem.at[s], rcv_sem.at[s], 2 * owner + s % 2)
+            remote(rin.at[s, owner], dst, fs_sem.at[s], rcv_sem.at[s], 2 * owner + s % 2, lat)
 
         @pl.when(core == s % 2)
         def _():
@@ -260,47 +250,66 @@
 
         @pl.when(core != s % 2)
         def _():
-            remote(rin.at[s, chip], dst, fs_sem.at[s], rcv_sem.at[s], 2 * chip + 1 - core)
+            remote(rin.at[s, chip], dst, fs_sem.at[s], rcv_sem.at[s], 2 * chip + 1 - core, lat)
+
+    behind = CHUNKS
+
+    def block(land):
+        pair = GROUP * (land // PARTS) + chip
+        return mu.at[pair, pl.ds(pl.multiple_of(PIECE * (land % PARTS), PIECE), PIECE)]
 
     def work(s):
-        side, chunk, flip = step_of(s)
-        row = pl.multiple_of(HALF * (chunk % 2), HALF)
+        chunk = chunk_at(s)
+        row = pl.multiple_of(PIECE * (chunk % PARTS), PIECE)
         pltpu.make_async_copy(rcv.at[s], rcv.at[s], rcv_sem.at[s]).wait()
         done = filter_chunk(
-            [rcv[s, d] for d in range(16)], table, lambda q: damp[side, q, pl.ds(row, HALF), :]
+            [rcv[s, d] for d in range(16)], table, lambda q: damp[q, pl.ds(row, PIECE), :]
         )
         for d in range(16):
             yout[s, d] = done[d]
-        land = landing(s)
-        pair = GROUP * (land // 2) + chip
-        dst = mu.at[pair, pl.ds(pl.multiple_of(HALF * (land % 2), HALF), HALF)]
+        relayed = jnp.where(over_y, behind + s, chunk)
+        relay_lat = jnp.where(over_y, lat, cap_lat)
         for k in range(1, 16):
             member = flip_bits(lon, k)
-            remote(yout.at[s, home_lon(member, flip)], dst, bs_sem.at[s], mu_sem.at[land], member)
-        pltpu.make_async_copy(yout.at[s, home_lon(lon, flip)], dst, mu_sem.at[land]).start()
+            land, land_lat = (relayed, relay_lat) if k & 8 else (chunk, cap_lat)
+            remote(yout.at[s, member], block(land), bs_sem.at[s], mu_sem.at[land], member, land_lat)
+
+        @pl.when(is_cap)
+        def _():
+            pltpu.make_async_copy(yout.at[s, lon], block(chunk), mu_sem.at[chunk]).start()
+
+        @pl.when(jnp.logical_not(is_cap))
+        def _():
+            remote(yout.at[s, lon], block(chunk), bs_sem.at[s], mu_sem.at[chunk], lon, cap_lat)
+
+    def pass_on(s):
+        pltpu.make_async_copy(rpass.at[s], rpass.at[s], rpass_sem.at[s]).wait()
+        remote(rpass.at[s], rin.at[s], pass_sem.at[s], rin_sem.at[s], lon, flip_bits(lat, 2, 3))
+
+    def half_of(ref, chunk):
+        pair = pl.multiple_of(GROUP * (chunk // PARTS) + 4 * (1 - chip // 4), 4)
+        row = pl.multiple_of(PIECE * (chunk % PARTS), PIECE)
+        return ref.at[pl.ds(pair, 4), pl.ds(row, PIECE)]
 
     def deliver(s):
-        side, chunk, flip = step_of(s)
-        part = chunk_of(mu, landing(s))
-        pltpu.make_async_copy(part, part, mu_sem.at[landing(s)]).wait()
-        pltpu.make_async_remote_copy(
-            src_ref=part, dst_ref=chunk_of(mu, chunk), send_sem=ro_sem.at[s], recv_sem=mu_sem.at[chunk],
-            device_id=to(home_lon(lon, flip), (LAT - 1) * side), device_id_type=MESH,
-        ).start()
+        chunk = chunk_at(s)
+        part = half_of(mu, behind + s)
+        pltpu.make_async_copy(part, part, mu_sem.at[behind + s]).wait()
+        remote(part, half_of(mu, chunk), ro_sem.at[s], mu_sem.at[chunk], lon, cap_lat)
 
     @pl.when(is_cap)
     def _():
-        turn = jnp.where(lower, 2, LAT - 2)
-        single, other = (lat + turn) % LAT, (lat + LAT - turn) % LAT
-        outer = to(mirror, flip_bits(lat, 1, 3))
-        for s in range(max(sum(SINGLE), sum(NEAR))):
-            if s < sum(NEAR):
-                relay(numbered(2, s, own_side), outer, 2 * s)
-                relay(numbered(3, s, own_side), to(lon, other), 2 * s + 1)
-            if s < sum(SINGLE):
-                relay(numbered(1, s, own_side), to(lon, single), s)
-
-        @pl.loop(0, sum(HOME))
+        targets = (
+            (1, to(lon, flip_bits(lat, 2, 3)), rin, rin_sem),
+            (2, to(lon, flip_bits(lat, 6, 3)), rin, rin_sem),
+            (3, to(mirror, flip_bits(lat, 1, 3)), rpass, rpass_sem),
+        )
+        for s in range(max(sum(kind) for kind in KINDS[1:])):
+            for kind, device, to_ref, to_sem in targets:
+                if s < sum(KINDS[kind]):
+                    relay(numbered(kind, s, own_side), device, to_ref, to_sem, s)
+
+        @pl.loop(0, AHEAD)
         def _(s):
             forward(s)
 
@@ -371,39 +380,44 @@
     col_at = lax.broadcasted_iota(jnp.int32, (ROWS, ROWS), 1)
     for copy in small_copies:
         copy.wait()
-    for side in range(2):
-        cut = cuts[side : side + 1, :].astype(jnp.float32)
-        column = jnp.sum(jnp.where(row_at == col_at, cut, 0.0), axis=1, keepdims=True)
-        for q in range(8):
-            damp[side, q] = jnp.minimum(1.0, column * column * inverse_k2[q : q + 1, :])
+    cut = jnp.where(own_side == 0, cuts[0:1, :], cuts[1:2, :]).astype(jnp.float32)
+    column = jnp.sum(jnp.where(row_at == col_at, cut, 0.0), axis=1, keepdims=True)
+    at = lax.broadcasted_iota(jnp.int32, (1, 2 * LANES), 1)
+    half = at % LANES
+    alone = jnp.where(at < LANES, 16 * jnp.where(half <= 64, half, half - 64), 16 * (half % 64) + 8)
+    for q in range(8):
+        freq = 16 * half + q
+        wave = alone if q == 0 else jnp.minimum(freq, NLON - freq)
+        damp[q] = jnp.minimum(1.0, (column / jnp.maximum(wave, 1).astype(jnp.float32)) ** 2)
+
+    lag = jnp.where(is_cap, 0, jnp.where(over_y, LAG, LEAD))
 
     @pl.loop(0, jnp.where(waves > 0, waves + lag, 0))
     def _(t):
-        for j in range(2):
-            @pl.when(helps & (t < waves) & (j < width))
-            def _():
-                forward(t * width + j)
-
-        s = jnp.where(is_double, (t - lead) * 2 + core, t - lead)
-
-        @pl.when((t >= lead) & (t < waves + lead) & (s % 2 == core))
+        passed = t + jnp.where(is_cap, AHEAD, 0)
+
+        @pl.when(passed < waves)
+        def _():
+            forward(passed)
+
+        @pl.when(is_far & (t < sum(NEAR)))
+        def _():
+            pass_on(t)
+
+        s = t - jnp.where(is_cap, 0, LEAD)
+
+        @pl.when((s >= 0) & (s < waves) & (s % 2 == core))
         def _():
             work(s)
 
-        for j in range(2):
-            @pl.when(helps & (t >= lag) & (j < width))
-            def _():
-                deliver((t - lag) * width + j)
+        @pl.when(over_y & (t >= LAG))
+        def _():
+            deliver(t - LAG)
 
     def arrived(chunk):
         part = chunk_of(mu, chunk)
         pltpu.make_async_copy(part, part, mu_sem.at[chunk]).wait()
 
-    def out_copy(first, count, sem):
-        return pltpu.make_async_copy(
-            mu.at[pl.ds(first, count)], mu_out.at[pl.ds(first, count)], local_sem.at[sem]
-        )
-
     early = 2 * CHUNKS // 3
 
     @pl.when(is_cap)
@@ -411,11 +425,9 @@
         for chunk in range(early):
             arrived(chunk)
         send_columns(mu, 1)
-        for group in range(CHUNKS // 6):
-            arrived(early + 2 * group + 1 - own_side)
+        for group in range(LEV // GROUP):
+            arrived(early + PARTS * group + (PARTS - 1) * (1 - own_side))
         send_rows(mu, 1)
-
-    out_copy(0, 2 * LEV, 5).start()
 
     for kind in range(2):
         for copy in ew_copies(kind):
@@ -461,39 +473,48 @@
 
     @pl.when(is_cap)
     def _():
-        for group in range(CHUNKS // 6):
-            arrived(early + 2 * group + own_side)
-
-    out_copy(2 * LEV, LEV, 6).start()
-
-    @pl.when(is_cap)
-    def _():
         for kind in (1, 2, 3):
-            for s in range(sum((HOME, SINGLE, NEAR, FAR)[kind])):
+            for s in range(sum(KINDS[kind])):
                 chunk = numbered(kind, s, own_side)
                 part = chunk_of(mu, chunk)
                 pltpu.make_async_copy(part, part, relay_sem.at[chunk]).wait()
 
-    @pl.loop(0, waves * width)
+    @pl.when(is_far)
+    def _():
+        for s in range(sum(NEAR)):
+            pltpu.make_async_copy(rpass.at[s], rpass.at[s], pass_sem.at[s]).wait()
+
+    @pl.loop(0, waves)
     def _(s):
         most = rin.at[s, pl.ds(0, 7)]
+        sent = rcv.at[s, pl.ds(0, 15)]
 
         @pl.when(core == s % 2)
         def _():
             pltpu.make_async_copy(most, most, fs_sem.at[s]).wait()
-            sent = rcv.at[s, pl.ds(0, 15)]
+
+        @pl.when(core != s % 2)
+        def _():
+            pltpu.make_async_copy(rin.at[s], rin.at[s], fs_sem.at[s]).wait()
+
+        @pl.when((core == s % 2) & is_cap)
+        def _():
             pltpu.make_async_copy(sent, sent, bs_sem.at[s]).wait()
 
-        @pl.when(core != s % 2)
-        def _():
-            pltpu.make_async_copy(rin.at[s], rin.at[s], fs_sem.at[s]).wait()
-
-        @pl.when(helps)
-        def _():
-            pltpu.make_async_copy(rin.at[s], rin.at[s], ro_sem.at[s]).wait()
-
-    out_copy(0, 2 * LEV, 5).wait()
-    out_copy(2 * LEV, LEV, 6).wait()
+        @pl.when((core == s % 2) & helps)
+        def _():
+            pltpu.make_async_copy(rcv.at[s], rcv.at[s], bs_sem.at[s]).wait()
+
+        @pl.when(over_y)
+        def _():
+            half = rin.at[s, pl.ds(0, 4)]
+            pltpu.make_async_copy(half, half, ro_sem.at[s]).wait()
+
+    @pl.when(is_cap)
+    def _():
+        for group in range(LEV // GROUP):
+            for part in range(PARTS - 1):
+                arrived(early + PARTS * group + part + own_side)
 
 
 LEVELS_STEP = 8
@@ -524,8 +545,8 @@
 
     for j in range(LEVELS_STEP):
         level = first + j
-        H, U, V = (traj[f, j] for f in range(3))
-        p, q, r = (mu[f, j] for f in range(3))
+        H, U, V = (traj[f * LEV + level] for f in range(3))
+        p, q, r = (mu[f * LEV + level] for f in range(3))
         x_h, x_u = fluxes(p, U, H, q, 1)
         y_h, y_v = fluxes(p, V, H, r, 0)
         over_h = jnp.where(edge, pltpu.roll(ew[...], (LANES - 2 * level) % LANES, axis=1), 0.0)
@@ -538,7 +559,7 @@
             out[2, j, at : at + 1, :] += ns[side, pl.ds(LEV + level, 1), :]
 
 
-TABLES, INVERSE_K2 = tables()
+TABLES = tables()
 
 
 def per_device(trajectory, adjoint_in, cutoffs):
@@ -547,57 +568,56 @@
     anywhere = pl.BlockSpec(memory_space=pl.ANY)
     vmem = pltpu.VMEM
     dma = pltpu.SemaphoreType.DMA
-    extra = GROUP * ((2 * sum(NEAR) + 1) // 2)
-    if sum(SINGLE) > 2 * sum(NEAR):
-        extra = GROUP * ((sum(SINGLE) + 1) // 2)
-    mu, ew, ns = pl.pallas_call(
+    extra = GROUP * ((max(sum(SINGLE), sum(FAR)) + PARTS - 1) // PARTS)
+    mu, trj, ew, ns = pl.pallas_call(
         exchange_kernel,
         out_shape=(
-            jax.ShapeDtypeStruct((PAIRS, ROWS, LANES), f32),
-            jax.ShapeDtypeStruct((ROWS, LANES), f32),
-            jax.ShapeDtypeStruct((2, 2 * LEV, LANES), f32),
-        ),
-        in_specs=[anywhere] * 5,
-        out_specs=(anywhere, whole, whole),
-        scratch_shapes=[
             vmem((PAIRS + extra, ROWS, LANES), f32),
             vmem((PAIRS, ROWS, LANES), f32),
-            vmem((SLOTS, GROUP, HALF, LANES), f32),
-            vmem((SLOTS, 16, HALF, LANES), f32),
-            vmem((SLOTS, 16, HALF, LANES), f32),
+            vmem((ROWS, LANES), f32),
+            vmem((2, 2 * LEV, LANES), f32),
+        ),
+        in_specs=[anywhere] * 4,
+        out_specs=(whole,) * 4,
+        scratch_shapes=[
+            vmem((sum(NEAR), GROUP, PIECE, LANES), f32),
+            vmem((SLOTS, GROUP, PIECE, LANES), f32),
+            vmem((SLOTS, 16, PIECE, LANES), f32),
+            vmem((SLOTS, 16, PIECE, LANES), f32),
             vmem((2, 2, 8, 256, 256), jnp.bfloat16),
-            vmem((2, 8, ROWS, 256), f32),
+            vmem((8, ROWS, 256), f32),
             vmem((2, ROWS), jnp.int32),
-            vmem((8, 256), f32),
             vmem((2, ROWS, LANES), f32),
             vmem((2, 2, ROWS, LANES), f32),
             vmem((2, 2, 2 * LEV, LANES), f32),
             vmem((2, 2, 2 * LEV, LANES), f32),
+            dma((sum(NEAR),)), dma((sum(NEAR),)),
             dma((SLOTS,)), dma((CHUNKS,)), dma((SLOTS,)), dma((SLOTS,)), dma((SLOTS,)), dma((SLOTS,)),
             dma((CHUNKS + SLOTS,)),
-            dma((2, 2)), dma((2, 2)), dma((2, 2)), dma((2, 2)), dma((7,)),
+            dma((2, 2)), dma((2, 2)), dma((2, 2)), dma((2, 2)), dma((4,)),
         ],
         compiler_params=pltpu.CompilerParams(
-            collective_id=0, has_side_effects=True, vmem_limit_bytes=48 << 20
+            collective_id=0, has_side_effects=True, vmem_limit_bytes=32 << 20
         ),
         name="exchange_filter",
-    )(
-        adjoint_in.reshape(PAIRS, ROWS, LANES),
-        trajectory.reshape(PAIRS, ROWS, LANES),
-        cutoffs,
-        jnp.asarray(INVERSE_K2),
-        jnp.asarray(TABLES),
-    )
-    field = pl.BlockSpec((3, LEVELS_STEP, ROWS, LANES), lambda i: (0, i, 0, 0))
+    )(*(
+        pltpu.with_memory_space_constraint(x, pltpu.HBM)
+        for x in (
+            adjoint_in.reshape(PAIRS, ROWS, LANES),
+            trajectory.reshape(PAIRS, ROWS, LANES),
+            cutoffs,
+            jnp.asarray(TABLES),
+        )
+    ))
     return pl.pallas_call(
         stencil_kernel,
         grid=(LEV // LEVELS_STEP,),
         out_shape=jax.ShapeDtypeStruct((3, LEV, ROWS, LANES), f32),
-        in_specs=[field, field, whole, whole],
-        out_specs=field,
+        in_specs=[whole] * 4,
+        out_specs=pl.BlockSpec((3, LEVELS_STEP, ROWS, LANES), lambda i: (0, i, 0, 0)),
         compiler_params=pltpu.CompilerParams(vmem_limit_bytes=24 << 20),
         name="adjoint_stencil",
-    )(trajectory, mu.reshape(3, LEV, ROWS, LANES), ew, ns)
+    )(*(pltpu.with_memory_space_constraint(x, pltpu.VMEM) for x in (trj, mu, ew, ns)))
 
 
 def solution(mesh):

time: 57.8 us -> 53.9 us (0.933)
  the two profiles are of different devices: /device:TPU:1 before, /device:TPU:24 now
where the time goes in v3:
time: 53.9 us; the launch traced here: 53.8 us
  Pallas kernels  53.8 us (100%)
    pallas_call x1, Pallas kernels, per_device(): pl.pallas_call(exchange_kernel, out_shape=(vmem((PAIRS + extra, ROWS, LAN...  48.7 us
    pallas_call x1, Pallas kernels, per_device(): pl.pallas_call(stencil_kernel, grid=(LEV // LEVELS_STEP,), out_shape=jax....  5.12 us

profile of v3, /device:TPU:24, one launch (start us, length us, event | category | flops | bytes accessed | tf_op | source)
XLA Modules:
  0.0 53.8 jit_solution(11659775252010669081)
XLA Ops:
  0.0 48.7 %exchange_filter.1 = (f32[120,64,128]{2,1,0:T(8,128)S(1)}, f32[96,64,128]{2,1,0:T(8,128)S(1)}, f32[64,128]{1,0:T(8,128)S(1)}, f32[2,64,128]{2,1,0:T(8,128)S(1)}) custom-call(f32[96,64,128]{2,1,0:T(8,128)} %bitcast.2, f32[96,64,128]{2,1,0:T(8,128)} %bitcast.3, s32[2,64]{1,0:T(2,128)} %cuts_in.1, bf16[2,2,8,256,256]{4,3,2,1,0:T(8,128)(2,1)} %constant.2.clone.table_in), custom_call_target="tpu_custom_call" | custom-call | tf_op jit(solution)/shard_map/exchange_filter/pallas_call | solution.py:572
  48.7 5.1 %adjoint_stencil.1 = f32[3,32,64,128]{3,2,1,0:T(8,128)} custom-call(f32[96,64,128]{2,1,0:T(8,128)S(1)} %get-tuple-element.9.traj, f32[120,64,128]{2,1,0:T(8,128)S(1)} %get-tuple-element.10.mu, f32[64,128]{1,0:T(8,128)S(1)} %get-tuple-element.11.ew, f32[2,64,128]{2,1,0:T(8,128)S(1)} %get-tuple-element.12.ns), custom_call_target="tpu_custom_call" | custom-call | tf_op jit(solution)/shard_map/adjoint_stencil/pallas_call | solution.py:612

commit v4 on v3

--- a/solution.py
+++ b/solution.py
@@ -19,6 +19,7 @@
 KINDS = (HOME, SINGLE, FAR, NEAR)
 SLOTS = max(sum(kind) for kind in KINDS)
 AHEAD, LEAD, LAG = 8, 1, 2
+WINDOW = 1
 cx, cy, cg, ca = 0.25, 0.25, 0.3, 0.25
 
 
@@ -219,12 +220,25 @@
 
     pl.semaphore_wait(barrier, len(peers))
 
-    def relay(chunk, device, to_ref, to_sem, slot):
+    targets = {
+        1: (to(lon, flip_bits(lat, 2, 3)), rin, rin_sem),
+        2: (to(lon, flip_bits(lat, 6, 3)), rin, rin_sem),
+        3: (to(mirror, flip_bits(lat, 1, 3)), rpass, rpass_sem),
+    }
+
+    def relay(kind, s):
+        device, to_ref, to_sem = targets[kind]
+        chunk = numbered(kind, s, own_side)
         pltpu.make_async_remote_copy(
-            src_ref=chunk_of(adj, chunk), dst_ref=to_ref.at[slot],
-            send_sem=relay_sem.at[chunk], recv_sem=to_sem.at[slot],
+            src_ref=chunk_of(adj, chunk), dst_ref=to_ref.at[s],
+            send_sem=relay_sem.at[chunk], recv_sem=to_sem.at[s],
             device_id=device, device_id_type=MESH,
         ).start()
+
+    def relayed_out(kind, s):
+        chunk = numbered(kind, s, own_side)
+        part = chunk_of(mu, chunk)
+        pltpu.make_async_copy(part, part, relay_sem.at[chunk]).wait()
 
     def chunk_at(s):
         return by_kind([numbered(kind, s, own_side) for kind in range(4)])
@@ -299,15 +313,10 @@
 
     @pl.when(is_cap)
     def _():
-        targets = (
-            (1, to(lon, flip_bits(lat, 2, 3)), rin, rin_sem),
-            (2, to(lon, flip_bits(lat, 6, 3)), rin, rin_sem),
-            (3, to(mirror, flip_bits(lat, 1, 3)), rpass, rpass_sem),
-        )
-        for s in range(max(sum(kind) for kind in KINDS[1:])):
-            for kind, device, to_ref, to_sem in targets:
+        for s in range(WINDOW):
+            for kind in (1, 2, 3):
                 if s < sum(KINDS[kind]):
-                    relay(numbered(kind, s, own_side), device, to_ref, to_sem, s)
+                    relay(kind, s)
 
         @pl.loop(0, AHEAD)
         def _(s):
@@ -394,21 +403,27 @@
 
     @pl.loop(0, jnp.where(waves > 0, waves + lag, 0))
     def _(t):
+        for kind in (1, 2, 3):
+            @pl.when(is_cap & (t < sum(KINDS[kind]) - WINDOW))
+            def _():
+                relayed_out(kind, t)
+                relay(kind, t + WINDOW)
+
         passed = t + jnp.where(is_cap, AHEAD, 0)
 
         @pl.when(passed < waves)
         def _():
             forward(passed)
 
+        s = t - jnp.where(is_cap, 0, LEAD)
+
+        @pl.when((s >= 0) & (s < waves) & (s % 2 == core))
+        def _():
+            work(s)
+
         @pl.when(is_far & (t < sum(NEAR)))
         def _():
             pass_on(t)
-
-        s = t - jnp.where(is_cap, 0, LEAD)
-
-        @pl.when((s >= 0) & (s < waves) & (s % 2 == core))
-        def _():
-            work(s)
 
         @pl.when(over_y & (t >= LAG))
         def _():
@@ -474,10 +489,8 @@
     @pl.when(is_cap)
     def _():
         for kind in (1, 2, 3):
-            for s in range(sum(KINDS[kind])):
-                chunk = numbered(kind, s, own_side)
-                part = chunk_of(mu, chunk)
-                pltpu.make_async_copy(part, part, relay_sem.at[chunk]).wait()
+            for s in range(max(sum(KINDS[kind]) - WINDOW, 0), sum(KINDS[kind])):
+                relayed_out(kind, s)
 
     @pl.when(is_far)
     def _():

time: 53.9 us -> 52.3 us (0.970)
  the two profiles are of different devices: /device:TPU:24 before, /device:TPU:1 now
where the time goes in v4:
time: 52.3 us; the launch traced here: 52.2 us
  Pallas kernels  52.2 us (100%)
    pallas_call x1, Pallas kernels, per_device(): pl.pallas_call(exchange_kernel, out_shape=(vmem((PAIRS + extra, ROWS, LAN...  47.1 us
    pallas_call x1, Pallas kernels, per_device(): pl.pallas_call(stencil_kernel, grid=(LEV // LEVELS_STEP,), out_shape=jax....  5.12 us

profile of v4, /device:TPU:1, one launch (start us, length us, event | category | flops | bytes accessed | tf_op | source)
XLA Modules:
  0.0 52.2 jit_solution(10139276628180918336)
XLA Ops:
  0.0 47.1 %exchange_filter.1 = (f32[120,64,128]{2,1,0:T(8,128)S(1)}, f32[96,64,128]{2,1,0:T(8,128)S(1)}, f32[64,128]{1,0:T(8,128)S(1)}, f32[2,64,128]{2,1,0:T(8,128)S(1)}) custom-call(f32[96,64,128]{2,1,0:T(8,128)} %bitcast.2, f32[96,64,128]{2,1,0:T(8,128)} %bitcast.3, s32[2,64]{1,0:T(2,128)} %cuts_in.1, bf16[2,2,8,256,256]{4,3,2,1,0:T(8,128)(2,1)} %constant.2.clone.table_in), custom_call_target="tpu_custom_call" | custom-call | tf_op jit(solution)/shard_map/exchange_filter/pallas_call | solution.py:585
  47.1 5.1 %adjoint_stencil.1 = f32[3,32,64,128]{3,2,1,0:T(8,128)} custom-call(f32[96,64,128]{2,1,0:T(8,128)S(1)} %get-tuple-element.9.traj, f32[120,64,128]{2,1,0:T(8,128)S(1)} %get-tuple-element.10.mu, f32[64,128]{1,0:T(8,128)S(1)} %get-tuple-element.11.ew, f32[2,64,128]{2,1,0:T(8,128)S(1)} %get-tuple-element.12.ns), custom_call_target="tpu_custom_call" | custom-call | tf_op jit(solution)/shard_map/adjoint_stencil/pallas_call | solution.py:625
